TPU v7x, 128 devices: a whole 4x4x4 slice. The times are simulated.
128 devices in a mesh: row: 8 (over y, core), col: 16 (over z, x).
Axes of the slice: x: 4, y: 4, z: 4, core: 2. Of those that a mesh axis runs over, the one named last changes fastest.
Arguments:
- object_field: float32 [2048, 2, 4096], P('row', None, 'col'), may hold values from -6 to 6
- probe_modes: float32 [4, 256, 2, 256], replicated, may hold values from -1.5 to 1.5
- amplitudes: bfloat16 [8, 128, 256, 256], P('row', 'col'), may hold values from 0 to 2
- positions: int32 [8, 128, 2], P('row', 'col'), may hold values from 0 to 4095, as said below
- counts: int32 [8, 16], P('row', 'col'), may hold values from 0 to 8, as said below
Outputs:
- update: float32 [2048, 2, 4096], P('row', None, 'col')
Inputs may be any that keep to these rules, and one draw needn't show every extreme that they name: counts[r, c] is the number of positions held by the owner at mesh row r, column c, in its first counts[r, c] slots. The 64 positions of row band r (object rows r * 256 to (r + 1) * 256 - 1) are held in scan order by the owners of mesh row r, owner 0 first, so the counts of a row sum to 64; in every row some owner holds exactly 8. A live slot's center lies in its owner's row band; exactly 4 centers of the band lie in each tile of it (tile columns c * 256 to (c + 1) * 256 - 1), and every center held by the owner in mesh column c lies in tile column c or c + 1. Entries of slots at or beyond an owner's count are not positions and are ignored.
All inputs are finite; a program needn't handle non-finite values.
Results may differ from a plain program's by a relative error of at most 0.0085.
Values may be sent and summed in bfloat16 or wider, within the bound.
A program may use at most 128 MiB of HBM per device.

v0:
```python
import jax
import jax.numpy as jnp
from jax import lax
from jax.sharding import PartitionSpec as P

floor_amplitude = 0.25
ridge_weight = 1.0


def padded(cells, sides, width):
    for axis, dim in sides:
        count = lax.axis_size(axis)
        ends = count - 1
        head = lax.slice_in_dim(cells, 0, width, axis=dim)
        tail = lax.slice_in_dim(cells, cells.shape[dim] - width, cells.shape[dim], axis=dim)
        cells = jnp.concatenate(
            [
                lax.ppermute(tail, axis, [(i, (i + 1) % count) for i in range(ends)]),
                cells,
                lax.ppermute(head, axis, [((i + 1) % count, i) for i in range(ends)]),
            ],
            axis=dim,
        )
    return cells


def from_behind(block, axis, distance):
    devices = range(lax.axis_size(axis))
    route = [(i - distance, i) for i in devices if i - distance in devices]
    return lax.ppermute(block, axis, route)


def dft_tables(extent):
    indices = jnp.arange(extent, dtype=jnp.int32)
    phase_steps = indices[:, None] * indices[None, :] % extent
    angles = phase_steps.astype(jnp.float32) * (2.0 * jnp.pi / extent)
    scaling = 1.0 / jnp.sqrt(jnp.float32(extent))
    cosine = (jnp.cos(angles) * scaling).astype(jnp.bfloat16)
    sine_table = (jnp.sin(angles) * scaling).astype(jnp.bfloat16)
    return (cosine, sine_table)


def transform_window(window, amplitude, probe_pair, cosine, sine_table):
    extent = window.shape[0]
    probe_re = probe_pair[:, :, :extent]
    probe_im = probe_pair[:, :, extent:]
    object_re = window[None, :, :extent]
    object_im = window[None, :, extent:]
    exit_wave = jnp.concatenate(
        [probe_re * object_re - probe_im * object_im, probe_re * object_im + probe_im * object_re],
        axis=-1,
    ).astype(jnp.bfloat16)
    forward_table = jnp.concatenate(
        [
            jnp.concatenate([cosine, -sine_table], axis=1),
            jnp.concatenate([sine_table, cosine], axis=1),
        ],
        axis=0,
    )
    inverse_table = jnp.concatenate(
        [
            jnp.concatenate([cosine, sine_table], axis=1),
            jnp.concatenate([-sine_table, cosine], axis=1),
        ],
        axis=0,
    )
    half_done = jnp.einsum(
        "kpq,qv->kpv", exit_wave, forward_table, preferred_element_type=jnp.float32
    ).astype(jnp.bfloat16)
    first_part = jnp.einsum("up,kpq->kuq", cosine, half_done, preferred_element_type=jnp.float32)
    second_part = jnp.einsum(
        "up,kpq->kuq", sine_table, half_done, preferred_element_type=jnp.float32
    )
    far_re = first_part[..., :extent] + second_part[..., extent:]
    far_im = first_part[..., extent:] - second_part[..., :extent]
    intensity = jnp.sum(far_re * far_re + far_im * far_im, axis=0)
    factor = 1.0 - amplitude.astype(jnp.float32) / jnp.maximum(jnp.sqrt(intensity), floor_amplitude)
    residue = jnp.concatenate([far_re * factor, far_im * factor], axis=-1).astype(jnp.bfloat16)
    first_back = jnp.einsum("up,kpq->kuq", cosine, residue, preferred_element_type=jnp.float32)
    second_back = jnp.einsum("up,kpq->kuq", sine_table, residue, preferred_element_type=jnp.float32)
    near_field = jnp.concatenate(
        [
            first_back[..., :extent] - second_back[..., extent:],
            first_back[..., extent:] + second_back[..., :extent],
        ],
        axis=-1,
    ).astype(jnp.bfloat16)
    returned = jnp.einsum(
        "kpq,qv->kpv", near_field, inverse_table, preferred_element_type=jnp.float32
    )
    back_re = returned[..., :extent]
    back_im = returned[..., extent:]
    grad_re = jnp.sum(probe_re * back_re + probe_im * back_im, axis=0)
    grad_im = jnp.sum(probe_re * back_im - probe_im * back_re, axis=0)
    return jnp.stack([grad_re, grad_im], axis=0)


def slot_gradients(windows, slot_amplitudes, probe_pair, cosine, sine_table, lighting):

    def slot_single(operands):
        gradient = transform_window(operands[0], operands[1], probe_pair, cosine, sine_table)
        return jnp.concatenate([gradient, lighting[None, :, :]], axis=0)

    return lax.map(slot_single, (windows, slot_amplitudes))


def cut_windows(extended, places, row_anchor, col_anchor, extent):

    def cut_single(location):
        corner = (jnp.int32(0), location[0] - row_anchor, location[1] - col_anchor)
        window = lax.dynamic_slice(extended, corner, (2, extent, extent))
        return jnp.concatenate([window[0], window[1]], axis=-1)

    return jax.vmap(cut_single)(places)


def add_windows(canvas, terms, places, row_anchor, col_anchor, weights):
    extent = terms.shape[-1]
    layers = terms.shape[1]

    def place(index, state):
        corner = (jnp.int32(0), places[index, 0] - row_anchor, places[index, 1] - col_anchor)
        current = lax.dynamic_slice(state, corner, (layers, extent, extent))
        return lax.dynamic_update_slice(state, current + terms[index] * weights[index], corner)

    return lax.fori_loop(0, terms.shape[0], place, canvas)


def fold_rim(spread, half_width, length, axis):
    middle = lax.slice_in_dim(spread, 2 * half_width, 2 * half_width + length, axis=axis)
    upper = lax.slice_in_dim(spread, 0, half_width, axis=axis)
    lower = lax.slice_in_dim(spread, length + 3 * half_width, length + 4 * half_width, axis=axis)
    widths = [(0, 0)] * spread.ndim
    top_pad = list(widths)
    top_pad[axis] = (0, length - half_width)
    low_pad = list(widths)
    low_pad[axis] = (length - half_width, 0)
    return middle + jnp.pad(upper, top_pad) + jnp.pad(lower, low_pad)


def on_device(object_field, probe_modes, amplitudes, positions, counts):
    extent = probe_modes.shape[1]
    half_width = extent // 2
    tile_rows = object_field.shape[0]
    tile_cols = object_field.shape[2]
    slot_count = amplitudes.shape[1]
    col_index = lax.axis_index("col")
    row_anchor = lax.axis_index("row") * tile_rows
    col_anchor = col_index * tile_cols
    cosine, sine_table = dft_tables(extent)
    probe_pair = probe_modes.reshape(probe_modes.shape[0], extent, 2 * extent)
    lighting = jnp.sum(probe_modes[:, :, 0, :] ** 2 + probe_modes[:, :, 1, :] ** 2, axis=0)
    planes = jnp.transpose(object_field, (1, 0, 2))
    extended = padded(planes, (("row", 1), ("col", 2)), half_width)
    own_positions = positions[0]
    own_amplitudes = amplitudes[0]
    own_count = counts[0]
    slot_numbers = jnp.arange(slot_count, dtype=jnp.int32)
    own_alive = slot_numbers < own_count[0]
    sent_numbers = jnp.arange(slot_count, dtype=jnp.int32)
    canvas = jnp.zeros((3, tile_rows + extent, tile_cols + extent), jnp.float32)
    left_positions, left_count = from_behind((own_positions, own_count), "col", 1)
    left_alive = sent_numbers < left_count[0]
    made_cuts = cut_windows(extended, left_positions, row_anchor, col_anchor, extent)
    from_right = from_behind(made_cuts, "col", -1)
    own_cuts = cut_windows(extended, own_positions, row_anchor, col_anchor, extent)
    at_home = own_positions[:, 1] // tile_cols == col_index
    windows = jnp.where(at_home[:, None, None], own_cuts, from_right)
    gradients = slot_gradients(windows, own_amplitudes, probe_pair, cosine, sine_table, lighting)
    home_live = own_alive & at_home
    canvas = add_windows(
        canvas, gradients, own_positions, row_anchor, col_anchor, home_live.astype(jnp.float32)
    )
    outgoing = gradients[:, :2, :, :]
    incoming = from_behind(outgoing.astype(jnp.bfloat16), "col", 1).astype(outgoing.dtype)
    lit_terms = jnp.broadcast_to(lighting[None, None, :, :], (slot_count, 1, extent, extent))
    left_live = left_alive & (left_positions[:, 1] // tile_cols == col_index)
    canvas = add_windows(
        canvas,
        jnp.concatenate([incoming, lit_terms], axis=1),
        left_positions,
        row_anchor,
        col_anchor,
        left_live.astype(jnp.float32),
    )
    spread = padded(canvas.astype(jnp.bfloat16), (("row", 1), ("col", 2)), half_width).astype(
        canvas.dtype
    )
    folded = fold_rim(fold_rim(spread, half_width, tile_rows, 1), half_width, tile_cols, 2)
    descent = folded[:2]
    weight = folded[2:]
    result = descent / (weight + ridge_weight)
    return jnp.transpose(result, (1, 0, 2))


def solution(mesh):
    in_specs = (
        P("row", None, "col"),
        P(),
        P("row", "col", None, None),
        P("row", "col", None),
        P("row", "col"),
    )
    out_specs = P("row", None, "col")
    return jax.shard_map(
        on_device, mesh=mesh, in_specs=in_specs, out_specs=out_specs, check_vma=False
    )
```

profile of v0, /device:TPU:15, one launch (start us, length us, event | category | flops | bytes accessed | tf_op | source)
XLA Modules:
  0.0 581.7 jit_solution(3194823670491792778)
XLA Ops:
  1.1 3.8 collective-permute-start
  6.9 3.5 collective-permute-start.4
  12.8 3.5 collective-permute-start.2
  18.2 9.6 %collective-permute-done.2 = f32[2,512,128]{2,1,0:T(8,128)S(1)} collective-permute-done((f32[2,512,128]{2,1,0:T(8,128)S(1)}, f32[2,512,128]{2,1,0:T(8,128)S(1)}, u32[]{:S(2)}, u32[]{:S(2)}) %collective-permute-start.2) | collective-permute-done | bytes 524320 | tf_op jit(solution)/shard_map/ppermute | solution.py:18
  28.6 4.8 collective-permute-done.3
  37.2 23.9 %while.45 = (s32[]{:T(128)}, f32[2,512,512]{2,1,0:T(8,128)S(1)}, s32[8,3]{0,1:T(4,128)S(1)}, f32[8,2,256,256]{3,2,0,1:T(8,128)}, s32[]{:T(128)}) while((s32[]{:T(128)}, f32[2,512,512]{2,1,0:T(8,128)S(1)}, s32[8,3]{0,1:T(4,128)S(1)}, f32[8,2,256,256]{3,2,0,1:T(8,128)}, s32[]{:T(128)}) %tuple.138), condition=%wide.while_cond.1, body=%wide.while_body.1.sunk | while | flops 2 | bytes 1050217 | solution.py:111
  61.1 3.3 slice_bitcast_fusion.1
  70.6 2.9 reshape.59
  77.2 3.9 add_reduce_fusion.2
  83.5 31.8 %while.44 = (s32[]{:T(128)}, f32[2,512,512]{2,1,0:T(8,128)}, s32[8,3]{0,1:T(4,128)S(1)}, f32[8,2,256,256]{3,2,0,1:T(8,128)}, s32[]{:T(128)}) while((s32[]{:T(128)}, f32[2,512,512]{2,1,0:T(8,128)}, s32[8,3]{0,1:T(4,128)S(1)}, f32[8,2,256,256]{3,2,0,1:T(8,128)}, s32[]{:T(128)}) %tuple.153), condition=%wide.while_cond, body=%wide.while_body.sunk | while | flops 2 | bytes 1050217 | solution.py:111
  84.1 3.4 bitcast_dynamic-update-slice_fusion.4
  88.2 3.4 bitcast_dynamic-update-slice_fusion.4
  92.2 3.4 bitcast_dynamic-update-slice_fusion.4
  96.2 3.4 bitcast_dynamic-update-slice_fusion.4
  100.2 3.3 bitcast_dynamic-update-slice_fusion.4
  104.2 3.3 bitcast_dynamic-update-slice_fusion.4
  108.1 3.3 bitcast_dynamic-update-slice_fusion.4
  112.1 3.3 bitcast_dynamic-update-slice_fusion.4
  118.0 45.3 %collective-permute-done.5 = f32[8,256,512]{2,1,0:T(8,128)} collective-permute-done((f32[8,256,512]{2,1,0:T(8,128)}, f32[8,256,512]{2,1,0:T(8,128)}, u32[]{:S(2)}, u32[]{:S(2)}) %collective-permute-start.5) | collective-permute-done | bytes 4194336 | tf_op jit(solution)/shard_map/ppermute | solution.py:30
  163.3 5.1 maximum_select_fusion
  168.4 99.6 %while.46 = (s32[]{:T(128)}, f32[8,3,256,256]{3,2,1,0:T(8,128)}, f32[4,256,512]{2,1,0:T(8,128)S(1)}, f32[8,256,512]{2,1,0:T(8,128)}, bf16[512,512]{1,0:T(8,128)(...) while((s32[]{:T(128)}, f32[8,3,256,256]{3,2,1,0:T(8,128)}, ...), condition=%wide.region_5.6_spmd.clone.clone, body=%wide.region_1.5_spmd.clone.clone.sunk | while | flops 2169438208 | bytes 50987676 | solution.py:104
  268.0 3.8 slice.338
  275.6 44.5 %collective-permute-done.7 = s32[1]{0:T(128)} collective-permute-done((s32[1]{0:T(128)}, s32[1]{0:T(128)}, u32[]{:S(2)}, u32[]{:S(2)}) %collective-permute-start.7) | collective-permute-done | bytes 36 | tf_op jit(solution)/shard_map/ppermute | solution.py:30
  322.9 104.3 %while.42 = (s32[]{:T(128)}, f32[3,512,512]{2,1,0:T(8,128)}, s32[8,2]{0,1:T(2,128)S(1)}, s32[]{:T(128)}, s32[]{:T(128)}, /*index=5*/f32[8,3,256,256]{3,2,1,0:T(8...) while((s32[]{:T(128)}, f32[3,512,512]{2,1,0:T(8,128)}, s32[8,2]{0,1:T(2,128)S(1)}, s32[]{:T(128)}, ...), condition=%wide.region_7.8_spmd, body=%wide.region_6.7_spmd.sunk | while | flops 393226 | bytes 3932405 | solution.py:126
  327.9 9.2 %dynamic_update_slice.26 = f32[3,512,512]{2,1,0:T(8,128)} dynamic-update-slice(f32[3,512,512]{2,1,0:T(8,128)} %get-tuple-element.824, f32[3,256,256]{2,1,0:T(8,128)S(1)} %bitcast_add_fusion.4, s32[]{:T(128)} %constant.134.clone.1..sunk, s32[]{:T(128)S(6)} %select_n.169, s32[]{:T(128)S(6)} %select_n.170) | dynamic-update-slice | bytes 1572868 | tf_op jit(solution)/shard_map/while/body/eval_jaxpr/dynamic_update_slice | solution.py:124
  342.0 9.3 %dynamic_update_slice.26 = f32[3,512,512]{2,1,0:T(8,128)} dynamic-update-slice(f32[3,512,512]{2,1,0:T(8,128)} %get-tuple-element.824, f32[3,256,256]{2,1,0:T(8,128)S(1)} %bitcast_add_fusion.4, s32[]{:T(128)} %constant.134.clone.1..sunk, s32[]{:T(128)S(6)} %select_n.169, s32[]{:T(128)S(6)} %select_n.170) | dynamic-update-slice | bytes 1572868 | tf_op jit(solution)/shard_map/while/body/eval_jaxpr/dynamic_update_slice | solution.py:124
  356.4 9.2 %dynamic_update_slice.26 = f32[3,512,512]{2,1,0:T(8,128)} dynamic-update-slice(f32[3,512,512]{2,1,0:T(8,128)} %get-tuple-element.824, f32[3,256,256]{2,1,0:T(8,128)S(1)} %bitcast_add_fusion.4, s32[]{:T(128)} %constant.134.clone.1..sunk, s32[]{:T(128)S(6)} %select_n.169, s32[]{:T(128)S(6)} %select_n.170) | dynamic-update-slice | bytes 1572868 | tf_op jit(solution)/shard_map/while/body/eval_jaxpr/dynamic_update_slice | solution.py:124
  370.6 8.6 %dynamic_update_slice.26 = f32[3,512,512]{2,1,0:T(8,128)} dynamic-update-slice(f32[3,512,512]{2,1,0:T(8,128)} %get-tuple-element.824, f32[3,256,256]{2,1,0:T(8,128)S(1)} %bitcast_add_fusion.4, s32[]{:T(128)} %constant.134.clone.1..sunk, s32[]{:T(128)S(6)} %select_n.169, s32[]{:T(128)S(6)} %select_n.170) | dynamic-update-slice | bytes 1572868 | tf_op jit(solution)/shard_map/while/body/eval_jaxpr/dynamic_update_slice | solution.py:124
  384.1 7.4 %dynamic_update_slice.26 = f32[3,512,512]{2,1,0:T(8,128)} dynamic-update-slice(f32[3,512,512]{2,1,0:T(8,128)} %get-tuple-element.824, f32[3,256,256]{2,1,0:T(8,128)S(1)} %bitcast_add_fusion.4, s32[]{:T(128)} %constant.134.clone.1..sunk, s32[]{:T(128)S(6)} %select_n.169, s32[]{:T(128)S(6)} %select_n.170) | dynamic-update-slice | bytes 1572868 | tf_op jit(solution)/shard_map/while/body/eval_jaxpr/dynamic_update_slice | solution.py:124
  396.3 7.3 %dynamic_update_slice.26 = f32[3,512,512]{2,1,0:T(8,128)} dynamic-update-slice(f32[3,512,512]{2,1,0:T(8,128)} %get-tuple-element.824, f32[3,256,256]{2,1,0:T(8,128)S(1)} %bitcast_add_fusion.4, s32[]{:T(128)} %constant.134.clone.1..sunk, s32[]{:T(128)S(6)} %select_n.169, s32[]{:T(128)S(6)} %select_n.170) | dynamic-update-slice | bytes 1572868 | tf_op jit(solution)/shard_map/while/body/eval_jaxpr/dynamic_update_slice | solution.py:124
  408.5 7.1 %dynamic_update_slice.26 = f32[3,512,512]{2,1,0:T(8,128)} dynamic-update-slice(f32[3,512,512]{2,1,0:T(8,128)} %get-tuple-element.824, f32[3,256,256]{2,1,0:T(8,128)S(1)} %bitcast_add_fusion.4, s32[]{:T(128)} %constant.134.clone.1..sunk, s32[]{:T(128)S(6)} %select_n.169, s32[]{:T(128)S(6)} %select_n.170) | dynamic-update-slice | bytes 1572868 | tf_op jit(solution)/shard_map/while/body/eval_jaxpr/dynamic_update_slice | solution.py:124
  420.5 6.7 %dynamic_update_slice.26 = f32[3,512,512]{2,1,0:T(8,128)} dynamic-update-slice(f32[3,512,512]{2,1,0:T(8,128)} %get-tuple-element.824, f32[3,256,256]{2,1,0:T(8,128)S(1)} %bitcast_add_fusion.4, s32[]{:T(128)} %constant.134.clone.1..sunk, s32[]{:T(128)S(6)} %select_n.169, s32[]{:T(128)S(6)} %select_n.170) | dynamic-update-slice | bytes 1572868 | tf_op jit(solution)/shard_map/while/body/eval_jaxpr/dynamic_update_slice | solution.py:124
  429.4 3.3 pad_maximum_fusion.3
  432.7 95.5 %while.43 = (s32[]{:T(128)}, f32[3,512,512]{2,1,0:T(8,128)}, s32[8,2]{0,1:T(2,128)S(1)}, s32[]{:T(128)}, s32[]{:T(128)}, /*index=5*/f32[8,3,256,256]{3,2,1,0:T(8...) while((s32[]{:T(128)}, f32[3,512,512]{2,1,0:T(8,128)}, s32[8,2]{0,1:T(2,128)S(1)}, s32[]{:T(128)}, ...), condition=%wide.region_9.10_spmd, body=%wide.region_8.9_spmd.sunk | while | flops 393226 | bytes 3932405 | solution.py:126
  437.5 7.4 %dynamic_update_slice.27 = f32[3,512,512]{2,1,0:T(8,128)} dynamic-update-slice(f32[3,512,512]{2,1,0:T(8,128)} %get-tuple-element.854, f32[3,256,256]{2,1,0:T(8,128)S(1)} %bitcast_add_fusion.5, s32[]{:T(128)} %constant.134.clone.1..sunk.1, s32[]{:T(128)S(6)} %select_n.171, s32[]{:T(128)S(6)} %select_n.172) | dynamic-update-slice | bytes 1572868 | tf_op jit(solution)/shard_map/while/body/eval_jaxpr/dynamic_update_slice | solution.py:124
  449.7 7.3 %dynamic_update_slice.27 = f32[3,512,512]{2,1,0:T(8,128)} dynamic-update-slice(f32[3,512,512]{2,1,0:T(8,128)} %get-tuple-element.854, f32[3,256,256]{2,1,0:T(8,128)S(1)} %bitcast_add_fusion.5, s32[]{:T(128)} %constant.134.clone.1..sunk.1, s32[]{:T(128)S(6)} %select_n.171, s32[]{:T(128)S(6)} %select_n.172) | dynamic-update-slice | bytes 1572868 | tf_op jit(solution)/shard_map/while/body/eval_jaxpr/dynamic_update_slice | solution.py:124
  461.8 7.2 %dynamic_update_slice.27 = f32[3,512,512]{2,1,0:T(8,128)} dynamic-update-slice(f32[3,512,512]{2,1,0:T(8,128)} %get-tuple-element.854, f32[3,256,256]{2,1,0:T(8,128)S(1)} %bitcast_add_fusion.5, s32[]{:T(128)} %constant.134.clone.1..sunk.1, s32[]{:T(128)S(6)} %select_n.171, s32[]{:T(128)S(6)} %select_n.172) | dynamic-update-slice | bytes 1572868 | tf_op jit(solution)/shard_map/while/body/eval_jaxpr/dynamic_update_slice | solution.py:124
  473.8 6.5 %dynamic_update_slice.27 = f32[3,512,512]{2,1,0:T(8,128)} dynamic-update-slice(f32[3,512,512]{2,1,0:T(8,128)} %get-tuple-element.854, f32[3,256,256]{2,1,0:T(8,128)S(1)} %bitcast_add_fusion.5, s32[]{:T(128)} %constant.134.clone.1..sunk.1, s32[]{:T(128)S(6)} %select_n.171, s32[]{:T(128)S(6)} %select_n.172) | dynamic-update-slice | bytes 1572868 | tf_op jit(solution)/shard_map/while/body/eval_jaxpr/dynamic_update_slice | solution.py:124
  485.1 7.4 %dynamic_update_slice.27 = f32[3,512,512]{2,1,0:T(8,128)} dynamic-update-slice(f32[3,512,512]{2,1,0:T(8,128)} %get-tuple-element.854, f32[3,256,256]{2,1,0:T(8,128)S(1)} %bitcast_add_fusion.5, s32[]{:T(128)} %constant.134.clone.1..sunk.1, s32[]{:T(128)S(6)} %select_n.171, s32[]{:T(128)S(6)} %select_n.172) | dynamic-update-slice | bytes 1572868 | tf_op jit(solution)/shard_map/while/body/eval_jaxpr/dynamic_update_slice | solution.py:124
  497.3 7.5 %dynamic_update_slice.27 = f32[3,512,512]{2,1,0:T(8,128)} dynamic-update-slice(f32[3,512,512]{2,1,0:T(8,128)} %get-tuple-element.854, f32[3,256,256]{2,1,0:T(8,128)S(1)} %bitcast_add_fusion.5, s32[]{:T(128)} %constant.134.clone.1..sunk.1, s32[]{:T(128)S(6)} %select_n.171, s32[]{:T(128)S(6)} %select_n.172) | dynamic-update-slice | bytes 1572868 | tf_op jit(solution)/shard_map/while/body/eval_jaxpr/dynamic_update_slice | solution.py:124
  509.6 6.7 %dynamic_update_slice.27 = f32[3,512,512]{2,1,0:T(8,128)} dynamic-update-slice(f32[3,512,512]{2,1,0:T(8,128)} %get-tuple-element.854, f32[3,256,256]{2,1,0:T(8,128)S(1)} %bitcast_add_fusion.5, s32[]{:T(128)} %constant.134.clone.1..sunk.1, s32[]{:T(128)S(6)} %select_n.171, s32[]{:T(128)S(6)} %select_n.172) | dynamic-update-slice | bytes 1572868 | tf_op jit(solution)/shard_map/while/body/eval_jaxpr/dynamic_update_slice | solution.py:124
  521.1 7.1 %dynamic_update_slice.27 = f32[3,512,512]{2,1,0:T(8,128)} dynamic-update-slice(f32[3,512,512]{2,1,0:T(8,128)} %get-tuple-element.854, f32[3,256,256]{2,1,0:T(8,128)S(1)} %bitcast_add_fusion.5, s32[]{:T(128)} %constant.134.clone.1..sunk.1, s32[]{:T(128)S(6)} %select_n.171, s32[]{:T(128)S(6)} %select_n.172) | dynamic-update-slice | bytes 1572868 | tf_op jit(solution)/shard_map/while/body/eval_jaxpr/dynamic_update_slice | solution.py:124
  530.4 14.0 %collective-permute-start.8 = (bf16[3,128,512]{2,1,0:T(8,128)(2,1)S(1)}, bf16[3,128,512]{2,1,0:T(8,128)(2,1)S(1)}, u32[]{:S(2)}, u32[]{:S(2)}) collective-permute-start(bf16[3,128,512]{2,1,0:T(8,128)(2,1)S(1)} %get-tuple-element.519), channel_id=1, source_target_pairs={{0,16},{16,32},{32,48},{48,64},{64,80},{80,96},{96,112},{1,17},{17... | collective-permute-start | bytes 1179656 | tf_op jit(solution)/shard_map/ppermute | solution.py:18
  546.3 2.8 collective-permute-done.8
  549.1 7.4 %collective-permute-done.9 = bf16[3,128,512]{2,1,0:T(8,128)(2,1)S(1)} collective-permute-done((bf16[3,128,512]{2,1,0:T(8,128)(2,1)S(1)}, bf16[3,128,512]{2,1,0:T(8,128)(2,1)S(1)}, u32[]{:S(2)}, u32[]{:S(2)}) %collective-permute-start.9) | collective-permute-done | bytes 393248 | tf_op jit(solution)/shard_map/ppermute | solution.py:20
  556.7 4.7 collective-permute-start.10
  563.3 9.6 %collective-permute-done.10 = bf16[3,768,128]{2,1,0:T(8,128)(2,1)S(1)} collective-permute-done((bf16[3,768,128]{2,1,0:T(8,128)(2,1)S(1)}, bf16[3,768,128]{2,1,0:T(8,128)(2,1)S(1)}, u32[]{:S(2)}, u32[]{:S(2)}) %collective-permute-start.10) | collective-permute-done | bytes 589856 | tf_op jit(solution)/shard_map/ppermute | solution.py:18
  572.9 6.2 %collective-permute-done.11 = bf16[3,768,128]{2,1,0:T(8,128)(2,1)S(1)} collective-permute-done((bf16[3,768,128]{2,1,0:T(8,128)(2,1)S(1)}, bf16[3,768,128]{2,1,0:T(8,128)(2,1)S(1)}, u32[]{:S(2)}, u32[]{:S(2)}) %collective-permute-start.11) | collective-permute-done | bytes 589856 | tf_op jit(solution)/shard_map/ppermute | solution.py:20
  (293 shorter events, 228.9 us)
Async XLA Ops:
  0.0 6.8 %copy-start.4 = (s32[1,8,2]{1,2,0:T(2,128)S(1)}, s32[1,8,2]{1,2,0:T(2,128)}, u32[]{:S(2)}) copy-start(s32[1,8,2]{1,2,0:T(2,128)} %param.14) | copy-start | bytes 196
  1.1 9.2 %collective-permute-start = (f32[2,128,256]{2,1,0:T(8,128)S(1)}, f32[2,128,256]{2,1,0:T(8,128)S(1)}, u32[]{:S(2)}, u32[]{:S(2)}) collective-permute-start(f32[2,128,256]{2,1,0:T(8,128)S(1)} %get-tuple-element.523), channel_id=1, source_target_pairs={{0,16},{16,32},{32,48},{48,64},{64,80},{80,96},{96,112},{1,17},{17... | collective-permute-start | bytes 786440 | tf_op jit(solution)/shard_map/ppermute | solution.py:18
  4.9 7.7 %collective-permute-start.1 = (f32[2,128,256]{2,1,0:T(8,128)S(1)}, f32[2,128,256]{2,1,0:T(8,128)S(1)}, u32[]{:S(2)}, u32[]{:S(2)}) collective-permute-start(f32[2,128,256]{2,1,0:T(8,128)S(1)} %get-tuple-element.524), channel_id=1, source_target_pairs={{16,0},{32,16},{48,32},{64,48},{80,64},{96,80},{112,96},{17,1},{33... | collective-permute-start | bytes 786440 | tf_op jit(solution)/shard_map/ppermute | solution.py:20
  6.9 11.3 %collective-permute-start.4 = (s32[8,2]{0,1:T(2,128)S(1)}, s32[8,2]{0,1:T(2,128)S(1)}, u32[]{:S(2)}, u32[]{:S(2)}) collective-permute-start(s32[8,2]{0,1:T(2,128)S(1)} %bitcast.178), channel_id=1, source_target_pairs={{0,1},{1,2},{2,3},{3,4},{4,5},{5,6},{6,7},{7,8},{8,9},{9,10},{10,1... | collective-permute-start | bytes 200 | tf_op jit(solution)/shard_map/ppermute | solution.py:30
  12.8 15.1 %collective-permute-start.2 = (f32[2,512,128]{2,1,0:T(8,128)S(1)}, f32[2,512,128]{2,1,0:T(8,128)S(1)}, u32[]{:S(2)}, u32[]{:S(2)}) collective-permute-start(f32[2,512,128]{2,1,0:T(8,128)S(1)} %get-tuple-element.521), channel_id=1, source_target_pairs={{0,1},{1,2},{2,3},{3,4},{4,5},{5,6},{6,7},{7,8},{8,9},{9,10},{10,1... | collective-permute-start | bytes 1572872 | tf_op jit(solution)/shard_map/ppermute | solution.py:18
  16.2 17.2 %collective-permute-start.3 = (f32[2,512,128]{2,1,0:T(8,128)S(1)}, f32[2,512,128]{2,1,0:T(8,128)}, u32[]{:S(2)}, u32[]{:S(2)}) collective-permute-start(f32[2,512,128]{2,1,0:T(8,128)S(1)} %get-tuple-element.522), channel_id=1, source_target_pairs={{1,0},{2,1},{3,2},{4,3},{5,4},{6,5},{7,6},{8,7},{9,8},{10,9},{11,1... | collective-permute-start | bytes 1572872 | tf_op jit(solution)/shard_map/ppermute | solution.py:20
  27.8 0.8 copy-start.3
  61.1 3.3 copy-start
  67.0 96.3 %collective-permute-start.5 = (f32[8,256,512]{2,1,0:T(8,128)}, f32[8,256,512]{2,1,0:T(8,128)}, u32[]{:S(2)}, u32[]{:S(2)}) collective-permute-start(f32[8,256,512]{2,1,0:T(8,128)} %pad_maximum_fusion.4), channel_id=1, source_target_pairs={{1,0},{2,1},{3,2},{4,3},{5,4},{6,5},{7,6},{8,7},{9,8},{10,9},{11,1... | collective-permute-start | bytes 12582920 | tf_op jit(solution)/shard_map/ppermute | solution.py:30
  169.5 1.0 copy-start.2
  177.7 1.0 copy-start.1
  182.0 1.0 copy-start.2
  190.2 1.0 copy-start.1
  194.5 1.0 copy-start.2
  202.7 1.0 copy-start.1
  206.9 1.0 copy-start.2
  215.1 1.0 copy-start.1
  219.4 1.0 copy-start.2
  227.5 1.0 copy-start.1
  231.8 1.0 copy-start.2
  240.0 1.0 copy-start.1
  244.2 1.0 copy-start.2
  252.4 1.0 copy-start.1
  256.7 1.0 copy-start.2
  264.9 1.0 copy-start.1
  271.8 155.4 %collective-permute-start.6 = (bf16[8,2,256,256]{3,2,1,0:T(8,128)(2,1)}, bf16[8,2,256,256]{3,2,1,0:T(8,128)(2,1)}, u32[]{:S(2)}, u32[]{:S(2)}) collective-permute-start(bf16[8,2,256,256]{3,2,1,0:T(8,128)(2,1)} %slice.338), channel_id=1, source_target_pairs={{0,1},{1,2},{2,3},{3,4},{4,5},{5,6},{6,7},{7,8},{8,9},{9,10},{10,1... | collective-permute-start | bytes 6291464 | tf_op jit(solution)/shard_map/ppermute | solution.py:30
  273.7 46.5 %collective-permute-start.7 = (s32[1]{0:T(128)}, s32[1]{0:T(128)}, u32[]{:S(2)}, u32[]{:S(2)}) collective-permute-start(s32[1]{0:T(128)} %bitcast.17), channel_id=1, source_target_pairs={{0,1},{1,2},{2,3},{3,4},{4,5},{5,6},{6,7},{7,8},{8,9},{9,10},{10,1... | collective-permute-start | bytes 20 | tf_op jit(solution)/shard_map/ppermute | solution.py:30
  530.4 18.7 %collective-permute-start.8 = (bf16[3,128,512]{2,1,0:T(8,128)(2,1)S(1)}, bf16[3,128,512]{2,1,0:T(8,128)(2,1)S(1)}, u32[]{:S(2)}, u32[]{:S(2)}) collective-permute-start(bf16[3,128,512]{2,1,0:T(8,128)(2,1)S(1)} %get-tuple-element.519), channel_id=1, source_target_pairs={{0,16},{16,32},{32,48},{48,64},{64,80},{80,96},{96,112},{1,17},{17... | collective-permute-start | bytes 1179656 | tf_op jit(solution)/shard_map/ppermute | solution.py:18
  544.4 12.1 %collective-permute-start.9 = (bf16[3,128,512]{2,1,0:T(8,128)(2,1)S(1)}, bf16[3,128,512]{2,1,0:T(8,128)(2,1)S(1)}, u32[]{:S(2)}, u32[]{:S(2)}) collective-permute-start(bf16[3,128,512]{2,1,0:T(8,128)(2,1)S(1)} %get-tuple-element.520), channel_id=1, source_target_pairs={{16,0},{32,16},{48,32},{64,48},{80,64},{96,80},{112,96},{17,1},{33... | collective-permute-start | bytes 1179656 | tf_op jit(solution)/shard_map/ppermute | solution.py:20
  556.7 16.2 %collective-permute-start.10 = (bf16[3,768,128]{2,1,0:T(8,128)(2,1)S(1)}, bf16[3,768,128]{2,1,0:T(8,128)(2,1)S(1)}, u32[]{:S(2)}, u32[]{:S(2)}) collective-permute-start(bf16[3,768,128]{2,1,0:T(8,128)(2,1)S(1)} %get-tuple-element.517), channel_id=1, source_target_pairs={{0,1},{1,2},{2,3},{3,4},{4,5},{5,6},{6,7},{7,8},{8,9},{9,10},{10,1... | collective-permute-start | bytes 1769480 | tf_op jit(solution)/shard_map/ppermute | solution.py:18
  561.3 17.8 %collective-permute-start.11 = (bf16[3,768,128]{2,1,0:T(8,128)(2,1)S(1)}, bf16[3,768,128]{2,1,0:T(8,128)(2,1)S(1)}, u32[]{:S(2)}, u32[]{:S(2)}) collective-permute-start(bf16[3,768,128]{2,1,0:T(8,128)(2,1)S(1)} %get-tuple-element.518), channel_id=1, source_target_pairs={{1,0},{2,1},{3,2},{4,3},{5,4},{6,5},{7,6},{8,7},{9,8},{10,9},{11,1... | collective-permute-start | bytes 1769480 | tf_op jit(solution)/shard_map/ppermute | solution.py:20
  579.2 0.7 copy-start.5
where the time goes:
time: 589 us; the launch traced here: 582 us
  local copies, waits for them, and re-layouts  242 us (41%)
  waiting for transfers between devices  132 us (22%)
  other arithmetic  86.2 us (15%)
  matrix products  56 us (10%)
  starting transfers between devices  42.8 us (7%)
  loops' own time  21 us (4%)
    dynamic_update_slice x16, local copies, waits for them, and re-layouts, place(): lax.dynamic_update_slice(state, current + terms[index] * weights[index],...  122 us
    ppermute x4, waiting for transfers between devices, from_behind(): return lax.ppermute(block, axis, route)  89.9 us
    gather x48, local copies, waits for them, and re-layouts  55.8 us
    add x16, other arithmetic, place(): current + terms[index] * weights[index]  36.9 us
    ppermute x4, starting transfers between devices, padded(): lax.ppermute(tail, axis, [(i, (i + 1) % count) for i in range(ends)])  25.9 us
    ppermute x4, waiting for transfers between devices, padded(): lax.ppermute(tail, axis, [(i, (i + 1) % count) for i in range(ends)])  22 us
    ppermute x4, waiting for transfers between devices, padded(): lax.ppermute(head, axis, [((i + 1) % count, i) for i in range(ends)])  20.6 us
    another operation x2, loops' own time, add_windows(): return lax.fori_loop(0, terms.shape[0], place, canvas)  20.4 us
  transfers between devices with their start and end apart: 12, of which 9 were waited for; matrix products, arithmetic and copies ran while one was open for 25% of the time, Pallas kernels for 0%

commit v1 on v0

v1 whole, which is shorter than its diff:
```python
import functools

import jax
import jax.numpy as jnp
import numpy as np
from jax import lax
from jax.experimental import pallas as pl
from jax.experimental.pallas import tpu as pltpu
from jax.sharding import PartitionSpec as P

MESH = pl.DeviceIdType.MESH
F32 = jnp.float32
BF16 = jnp.bfloat16

floor_amplitude = 0.25
ridge_weight = 1.0

POS, CNT = 0, 1
OBJ_X = 2
OBJ_Y = 4
CORNER = 6
AMP = 10
W_Y = 14
W_X = 16
G_Y = 18
G_X = 22
COPIES = 26


def tables(extent):
    half = extent // 2
    steps = np.arange(extent)
    turns = np.outer(np.arange(half), steps) % extent
    scale = 1.0 / np.sqrt(extent)
    cosine = np.cos(2.0 * np.pi * turns / extent) * scale
    sine = np.sin(2.0 * np.pi * turns / extent) * scale
    forward = []
    for parity in range(2):
        c, s = cosine[:, parity::2], sine[:, parity::2]
        forward.append(np.block([[c, -s], [s, c]]))
    order = np.concatenate([steps[0::2], steps[1::2]])
    permute = np.eye(extent)[order]
    stack = [forward[0], forward[1], forward[0].T, forward[1].T, permute, permute.T]
    return np.stack(stack).astype(np.float32).astype(jnp.bfloat16)


def dot(a, b):
    return jnp.dot(a, b, preferred_element_type=F32)


def kernel(
    n_row, n_col, slots, modes,
    obj_hbm, probe_hbm, amp_hbm, tab_hbm, pos, cnt, out,
    obj, probe, amps, tab, pp, light, ext, win,
    sx, rx, sy, ry, rc, sa, ra, left_pos, left_cnt, table,
    far, fac, grad, pg, pw, cv, cw,
    wsy, wry, wsx, wrx, gsy, gry, gsx, grx,
    lsem, ssem, rsem,
):
    row, col = lax.axis_index("row"), lax.axis_index("col")
    right, left = lax.rem(col + 1, n_col), lax.rem(col + n_col - 1, n_col)
    down, up = lax.rem(row + 1, n_row), lax.rem(row + n_row - 1, n_row)
    to_right, to_left, to_down, to_up = (row, right), (row, left), (down, col), (up, col)

    def remote(number, src, dst, target):
        return pltpu.make_async_remote_copy(
            src_ref=src, dst_ref=dst, send_sem=ssem.at[number], recv_sem=rsem.at[number],
            device_id=target, device_id_type=MESH,
        )

    local = [
        pltpu.make_async_copy(obj_hbm, obj, lsem.at[0]),
        pltpu.make_async_copy(amp_hbm, amps.at[pl.ds(0, slots)], lsem.at[1]),
        pltpu.make_async_copy(probe_hbm, probe, lsem.at[2]),
        pltpu.make_async_copy(tab_hbm, tab, lsem.at[3]),
    ]
    for copy in local:
        copy.start()

    barrier = pltpu.get_barrier_semaphore()
    for target in (to_right, to_left, to_down, to_up):
        pl.semaphore_signal(barrier, inc=1, device_id=target, device_id_type=MESH)

    local[0].wait()
    for c in range(2):
        for b in range(2):
            ext[c, 1 + b, 128:384, :] = obj[pl.ds(2 * b + c, 256, stride=4), :]
    for c in range(2):
        sx[0, c] = ext[c, 2, 128:384, :].astype(BF16)
        sx[1, c] = ext[c, 1, 128:384, :].astype(BF16)
    for c in range(2):
        for b in range(2):
            sy[0, c, b] = ext[c, 1 + b, 256:384, :].astype(BF16)
            sy[1, c, b] = ext[c, 1 + b, 128:256, :].astype(BF16)

    pl.semaphore_wait(barrier, 4)
    sent = []

    def send(*arguments):
        copy = remote(*arguments)
        copy.start()
        sent.append(copy)
        return copy

    pos_copy = send(POS, pos, left_pos, to_right)
    cnt_copy = send(CNT, cnt, left_cnt, to_right)
    obj_x = [send(OBJ_X, sx.at[0], rx.at[0], to_right), send(OBJ_X + 1, sx.at[1], rx.at[1], to_left)]
    obj_y = [send(OBJ_Y, sy.at[0], ry.at[0], to_down), send(OBJ_Y + 1, sy.at[1], ry.at[1], to_up)]

    def ranked(ref, count, tile):
        rank = jnp.int32(0)
        picked = [[jnp.int32(0)] * 3 for _ in range(4)]
        for i in range(slots):
            y, x = ref[0, i, 0], ref[0, i, 1]
            here = jnp.where((i < count) & ((x >> 8) == tile), 1, 0)
            for j in range(4):
                hit = jnp.where(rank == j, here, 0)
                picked[j] = [old + hit * new for old, new in zip(picked[j], (i, y, x))]
            rank = rank + here
        return picked, rank

    going, _ = ranked(pos, cnt[0, 0], col + 1)
    local[1].wait()
    for j in range(4):
        sa[j] = amps[going[j][0] & (slots - 1)]
    for j in range(4):
        send(AMP + j, sa.at[j], ra.at[j], to_right)

    local[2].wait()
    for k in range(modes):
        for c in range(2):
            for b in range(2):
                pp[k, c, b] = probe[pl.ds(k * 1024 + 2 * b + c, 256, stride=4), :]
    for b in range(2):
        total = None
        for k in range(modes):
            for c in range(2):
                term = pp[k, c, b] * pp[k, c, b]
                total = term if total is None else total + term
        light[b] = total

    pg[...] = jnp.zeros_like(pg)
    pw[...] = jnp.zeros_like(pw)
    cv[...] = jnp.zeros_like(cv)
    cw[...] = jnp.zeros_like(cw)
    for j in range(4):
        amps[slots + j] = jnp.zeros((256, 256), BF16)

    pos_copy.wait_recv()
    cnt_copy.wait_recv()
    home, n_home = ranked(pos, cnt[0, 0], col)
    came, _ = ranked(left_pos, left_cnt[0, 0], col)
    for j in range(4):
        for i in range(2):
            table[3 + i, j] = came[j][1 + i]
    for j in range(4):
        from_left = j >= n_home
        there = jnp.clip(j - n_home, 0, 3)
        table[0, j] = jnp.where(from_left, slots + there, home[j][0])
        for i in range(2):
            table[1 + i, j] = jnp.where(from_left, table[3 + i, there], home[j][1 + i]) & 255

    corners = []
    for side in range(2):
        obj_x[side].wait_recv()
        corners.append(send(CORNER + side, rx.at[side, :, pl.ds(128, 128)], rc.at[0, side], to_down))
        corners.append(send(CORNER + 2 + side, rx.at[side, :, pl.ds(0, 128)], rc.at[1, side], to_up))

    lanes = lax.broadcasted_iota(jnp.int32, (256, 128), 1)

    def spread(ref, pieces, shift):
        keep = lanes >= shift
        low, high = (pltpu.roll(piece, shift, 1) for piece in pieces)
        ref[1, 256:512, :] = jnp.where(keep, low, 0.0)
        ref[2, 256:512, :] = jnp.where(keep, high, low)
        ref[3, 256:512, :] = jnp.where(keep, 0.0, high)

    def place(canvas, ref, y, block):
        for b in range(4):
            canvas[b] += ref[b - block + 1, pl.ds(256 - y, 512), :]

    def weigh(j, carry):
        y, x = table[1, j], table[2, j]
        spread(pw, [light[0], light[1]], x & 127)
        place(cw, pw, y, x >> 7)
        return carry

    lax.fori_loop(0, 4, weigh, 0)
    for b in range(4):
        wsy[0, b] = cw[b, 384:512, :].astype(BF16)
        wsy[1, b] = cw[b, 0:128, :].astype(BF16)
    w_y = [send(W_Y, wsy.at[0], wry.at[0], to_down), send(W_Y + 1, wsy.at[1], wry.at[1], to_up)]

    from_left_on = jnp.where(col > 0, 1.0, 0.0).astype(F32)
    from_right_on = jnp.where(col < n_col - 1, 1.0, 0.0).astype(F32)
    from_up_on = jnp.where(row > 0, 1.0, 0.0).astype(F32)
    from_down_on = jnp.where(row < n_row - 1, 1.0, 0.0).astype(F32)
    x_on, y_on = (from_left_on, from_right_on), (from_up_on, from_down_on)
    for side in range(2):
        for c in range(2):
            ext[c, 3 * side, 128:384, :] = rx[side, c].astype(F32) * x_on[side]
    for end in range(2):
        obj_y[end].wait_recv()
        first = 384 * end
        for c in range(2):
            for b in range(2):
                ext[c, 1 + b, first : first + 128, :] = ry[end, c, b].astype(F32) * y_on[end]
    for copy in corners:
        copy.wait_recv()
    for end in range(2):
        first = 384 * end
        for side in range(2):
            for c in range(2):
                ext[c, 3 * side, first : first + 128, :] = rc[end, side, c].astype(F32) * (y_on[end] * x_on[side])

    local[3].wait()

    def slot(j, carry):
        y, x = table[1, j], table[2, j]
        block, shift = x >> 7, x & 127
        keep = lanes >= shift
        for c in range(2):
            for b in range(2):
                near = ext[c, block + b, pl.ds(y, 256), :]
                far_off = ext[c, block + b + 1, pl.ds(y, 256), :]
                win[c, b] = pltpu.roll(jnp.where(keep, near, far_off), (128 - shift) & 127, 1)
        for k in range(modes):
            waves = []
            for b in range(2):
                p_re, p_im, w_re, w_im = pp[k, 0, b], pp[k, 1, b], win[0, b], win[1, b]
                waves.append((p_re * w_re - p_im * w_im, p_re * w_im + p_im * w_re))
            (lo_re, lo_im), (hi_re, hi_im) = waves
            even = jnp.concatenate([lo_re + hi_re, lo_im + hi_im], axis=1).astype(BF16)
            odd = jnp.concatenate([lo_re - hi_re, lo_im - hi_im], axis=1).astype(BF16)
            h_even, h_odd = dot(even, tab[0]), dot(odd, tab[1])
            for parity in range(2):
                if parity == 0:
                    e, o = h_even[:128] + h_even[128:], h_odd[:128] + h_odd[128:]
                else:
                    e, o = h_even[:128] - h_even[128:], h_odd[:128] - h_odd[128:]
                stacked = jnp.concatenate(
                    [
                        jnp.concatenate([e[:, :128], o[:, :128]], axis=1),
                        jnp.concatenate([e[:, 128:], o[:, 128:]], axis=1),
                    ],
                    axis=0,
                ).astype(BF16)
                far[parity, k] = dot(tab[2 + parity], stacked)

        pltpu.make_async_remote_copy(
            src_ref=sa.at[j], dst_ref=ra.at[j], send_sem=ssem.at[AMP + j], recv_sem=rsem.at[AMP + j],
            device_id=to_right, device_id_type=MESH,
        ).wait_recv()
        amps[slots + j] = ra[j]
        rows_split = dot(tab[4], amps[table[0, j]]).astype(BF16)
        amplitude = dot(rows_split, tab[5])
        for parity in range(2):
            intensity = None
            for k in range(modes):
                re, im = far[parity, k, :128, :], far[parity, k, 128:, :]
                term = re * re + im * im
                intensity = term if intensity is None else intensity + term
            held = lax.rsqrt(jnp.maximum(intensity, floor_amplitude * floor_amplitude))
            fac[parity] = 1.0 - amplitude[128 * parity : 128 * parity + 128] * held

        for k in range(modes):
            parts = []
            for parity in range(2):
                factor = jnp.concatenate([fac[parity], fac[parity]], axis=0)
                parts.append(dot(tab[parity], (far[parity, k] * factor).astype(BF16)))
            low, high = parts[0] + parts[1], parts[0] - parts[1]
            ends = []
            for parity in range(2):
                cut = slice(128 * parity, 128 * parity + 128)
                near = jnp.concatenate(
                    [
                        jnp.concatenate([low[:128, cut], low[128:, cut]], axis=1),
                        jnp.concatenate([high[:128, cut], high[128:, cut]], axis=1),
                    ],
                    axis=0,
                ).astype(BF16)
                ends.append(dot(near, tab[2 + parity]))
            for b in range(2):
                back = ends[0] + ends[1] if b == 0 else ends[0] - ends[1]
                b_re, b_im = back[:, :128], back[:, 128:]
                p_re, p_im = pp[k, 0, b], pp[k, 1, b]
                g_re, g_im = p_re * b_re + p_im * b_im, p_re * b_im - p_im * b_re
                if k == 0:
                    grad[0, b], grad[1, b] = g_re, g_im
                else:
                    grad[0, b] += g_re
                    grad[1, b] += g_im
        for c in range(2):
            spread(pg.at[c], [grad[c, 0], grad[c, 1]], shift)
            place(cv.at[c], pg.at[c], y, block)
        return carry

    lax.fori_loop(0, 4, slot, 0)

    g_y = []
    for c in range(2):
        for b in range(4):
            gsy[c, 0, b] = cv[c, b, 384:512, :].astype(BF16)
            gsy[c, 1, b] = cv[c, b, 0:128, :].astype(BF16)
        g_y.append(send(G_Y + 2 * c, gsy.at[c, 0], gry.at[c, 0], to_down))
        g_y.append(send(G_Y + 2 * c + 1, gsy.at[c, 1], gry.at[c, 1], to_up))

    for copy in w_y:
        copy.wait_recv()
    for end in range(2):
        cut = slice(128 + 128 * end, 256 + 128 * end)
        for b in range(4):
            cw[b, cut, :] += wry[end, b].astype(F32) * y_on[end]
    wsx[0] = cw[3, 128:384, :].astype(BF16)
    wsx[1] = cw[0, 128:384, :].astype(BF16)
    w_x = [send(W_X, wsx.at[0], wrx.at[0], to_right), send(W_X + 1, wsx.at[1], wrx.at[1], to_left)]

    g_x = []
    for c in range(2):
        for end in range(2):
            g_y[2 * c + end].wait_recv()
            cut = slice(128 + 128 * end, 256 + 128 * end)
            for b in (0, 3):
                side = 0 if b == 3 else 1
                piece = cv[c, b, cut, :] + gry[c, end, b].astype(F32) * y_on[end]
                gsx[c, side, 128 * end : 128 * end + 128, :] = piece.astype(BF16)
        g_x.append(send(G_X + 2 * c, gsx.at[c, 0], grx.at[c, 0], to_right))
        g_x.append(send(G_X + 2 * c + 1, gsx.at[c, 1], grx.at[c, 1], to_left))
        for end in range(2):
            cut = slice(128 + 128 * end, 256 + 128 * end)
            for b in (1, 2):
                cv[c, b, cut, :] += gry[c, end, b].astype(F32) * y_on[end]
    for b in range(2):
        w_x[b].wait_recv()
        weight = cw[1 + b, 128:384, :] + wrx[b].astype(F32) * x_on[b]
        cw[1 + b, 128:384, :] = 1.0 / (weight + ridge_weight)
    for c in range(2):
        for b in range(2):
            g_x[2 * c + b].wait_recv()
            total = cv[c, 1 + b, 128:384, :] + grx[c, b].astype(F32) * x_on[b]
            out[pl.ds(2 * b + c, 256, stride=4), :] = total * cw[1 + b, 128:384, :]

    for copy in sent:
        copy.wait_send()


def on_device(n_row, n_col, object_field, probe_modes, amplitudes, positions, counts):
    modes, extent = probe_modes.shape[0], probe_modes.shape[1]
    slots = amplitudes.shape[1]
    half = extent // 2
    obj = object_field.reshape(extent, 2, 2, half).transpose(0, 2, 1, 3).reshape(4 * extent, half)
    probe = probe_modes.reshape(modes, extent, 2, 2, half).transpose(0, 1, 3, 2, 4)
    probe = probe.reshape(modes * 4 * extent, half)
    tab = jnp.asarray(tables(extent))
    big = 2 * extent
    vmem, anywhere = pltpu.VMEM, pl.BlockSpec(memory_space=pl.ANY)
    scratch = [
        vmem((4 * extent, half), F32),
        vmem((modes * 4 * extent, half), F32),
        vmem((slots + 4, extent, extent), BF16),
        vmem((6, extent, extent), BF16),
        vmem((modes, 2, 2, extent, half), F32),
        vmem((2, extent, half), F32),
        vmem((2, 4, big, half), F32),
        vmem((2, 2, extent, half), F32),
        vmem((2, 2, extent, half), BF16),
        vmem((2, 2, extent, half), BF16),
        vmem((2, 2, 2, half, half), BF16),
        vmem((2, 2, 2, half, half), BF16),
        vmem((2, 2, 2, half, half), BF16),
        vmem((4, extent, extent), BF16),
        vmem((4, extent, extent), BF16),
        pltpu.SMEM((1, slots, 2), jnp.int32),
        pltpu.SMEM((1, 1), jnp.int32),
        pltpu.SMEM((5, 4), jnp.int32),
        vmem((2, modes, extent, extent), F32),
        vmem((2, half, extent), F32),
        vmem((2, 2, extent, half), F32),
        vmem((2, 5, 3 * extent, half), F32),
        vmem((5, 3 * extent, half), F32),
        vmem((2, 4, big, half), F32),
        vmem((4, big, half), F32),
        vmem((2, 4, half, half), BF16),
        vmem((2, 4, half, half), BF16),
        vmem((2, extent, half), BF16),
        vmem((2, extent, half), BF16),
        vmem((2, 2, 4, half, half), BF16),
        vmem((2, 2, 4, half, half), BF16),
        vmem((2, 2, extent, half), BF16),
        vmem((2, 2, extent, half), BF16),
        pltpu.SemaphoreType.DMA((4,)),
        pltpu.SemaphoreType.DMA((COPIES,)),
        pltpu.SemaphoreType.DMA((COPIES,)),
    ]
    update = pl.pallas_call(
        functools.partial(kernel, n_row, n_col, slots, modes),
        out_shape=jax.ShapeDtypeStruct((4 * extent, half), F32),
        in_specs=[anywhere] * 4 + [pl.BlockSpec(memory_space=pltpu.SMEM)] * 2,
        out_specs=pl.BlockSpec(memory_space=pltpu.VMEM),
        scratch_shapes=scratch,
        compiler_params=pltpu.CompilerParams(
            collective_id=0, has_side_effects=True, vmem_limit_bytes=56 * 1024 * 1024
        ),
        cost_estimate=pl.CostEstimate(flops=5 * 10**9, bytes_accessed=5 * 10**6, transcendentals=3 * 10**5),
    )(obj, probe, amplitudes[0], tab, positions, counts)
    return update.reshape(extent, 2, 2, half).transpose(0, 2, 1, 3).reshape(extent, 2, extent)


def solution(mesh):
    in_specs = (
        P("row", None, "col"),
        P(),
        P("row", "col", None, None),
        P("row", "col", None),
        P("row", "col"),
    )
    out_specs = P("row", None, "col")
    step = functools.partial(on_device, mesh.shape["row"], mesh.shape["col"])
    return jax.shard_map(step, mesh=mesh, in_specs=in_specs, out_specs=out_specs, check_vma=False)
```

time: 589 us -> 46.5 us (0.08)
  the two profiles are of different devices: /device:TPU:15 before, /device:TPU:0 now
where the time goes in v1:
time: 46.5 us; the launch traced here: 46.3 us
  Pallas kernels  42.3 us (91%)
  local copies, waits for them, and re-layouts  3.36 us (7%)
  between operations  0.66 us (1%)
    pallas_call x1, Pallas kernels, on_device(): pl.pallas_call(functools.partial(kernel, n_row, n_col, slots, modes), out...  42.3 us
    unnamed x2, local copies, waits for them, and re-layouts  3.36 us

profile of v1, /device:TPU:0, one launch (start us, length us, event | category | flops | bytes accessed | tf_op | source)
XLA Modules:
  0.0 46.3 jit_solution(14718559189268492712)
XLA Ops:
  0.7 1.3 %copy.9.pos = s32[1,8,2]{2,1,0:T(8,128)} copy(s32[1,8,2]{1,2,0:T(2,128)} %param.9) | data formatting | bytes 128 | tf_op args[3]
  2.0 42.3 %shard_map.64 = f32[1024,128]{1,0:T(8,128)} custom-call(f32[1024,128]{1,0:T(8,128)} %bitcast.19, f32[4096,128]{1,0:T(8,128)} %bitcast.17, bf16[8,256,256]{2,1,0:T(8,128)(2,1)} %bitcast.18, bf16[6,256,256]{2,1,0:T(8,128)(2,1)} %constant.2.clone.tab_hbm, s32[1,8,2]{2,1,0:T(8,128)} %copy.9.pos, s32[1,1]{1,0:T(1,128)S(6)} %copy.12.cnt), custom_call_target="tpu_custom_call" | custom-call | flops 5000000000 | bytes 5000000 | tf_op jit(solution)/shard_map/pallas_call | solution.py:395
  44.3 2.0 %copy.13 = f32[256,2,256]{2,1,0:T(2,128)} copy(f32[256,2,256]{2,1,0:T(2,128)} %bitcast.16) | data formatting | bytes 1048576

commit v2 on v1

v2 whole, which is shorter than its diff:
```python
import functools

import jax
import jax.numpy as jnp
import numpy as np
from jax import lax
from jax.experimental import pallas as pl
from jax.experimental.pallas import tpu as pltpu
from jax.sharding import PartitionSpec as P

MESH = pl.DeviceIdType.MESH
F32 = jnp.float32
BF16 = jnp.bfloat16

floor_amplitude = 0.25
ridge_weight = 1.0

POS, CNT = 0, 1
OBJ = 2
CORNER = 8
AMP = 12
WEIGHT = 16
GRAD = 24
COPIES = 32
RIGHT, LEFT = (0, 1), (0, -1)


def tables(extent):
    half = extent // 2
    steps = np.arange(extent)
    turns = np.outer(np.arange(half), steps) % extent
    scale = 1.0 / np.sqrt(extent)
    cosine = np.cos(2.0 * np.pi * turns / extent) * scale
    sine = np.sin(2.0 * np.pi * turns / extent) * scale
    forward = []
    for parity in range(2):
        c, s = cosine[:, parity::2], sine[:, parity::2]
        forward.append(np.block([[c, -s], [s, c]]))
    order = np.concatenate([steps[0::2], steps[1::2]])
    permute = np.eye(extent)[order]
    stack = [forward[0], forward[1], forward[0].T, forward[1].T, permute, permute.T]
    return np.stack(stack).astype(np.float32).astype(jnp.bfloat16)


def dot(a, b):
    return jnp.dot(a, b, preferred_element_type=F32)


def kernel(
    n_row, n_col, slots, modes,
    obj_hbm, probe_hbm, amp_hbm, tab_hbm, pos, cnt, out,
    obj, probe, amps, tab, pp, light, ext, win,
    rim, sa, ra, left_pos, left_cnt, table,
    far, fac, grad, pg, pw, cv, cw,
    ws, wi, wx, wd, wo, gs, gi, gx, gd, go,
    lsem, ssem, rsem,
):
    row, col = lax.axis_index("row"), lax.axis_index("col")
    core = lax.rem(row, 2)
    outer, inner = 2 * core - 1, 1 - 2 * core
    has = {
        "right": col < n_col - 1, "left": col > 0,
        "outer": jnp.where(core == 0, row > 0, row < n_row - 1), "inner": row >= 0,
    }
    sides = (("right", 1), ("left", -1))

    def to(vertical, across):
        step = {"outer": outer, "inner": inner, "": 0}[vertical]
        return (row + step, col + {"right": 1, "left": -1, "": 0}[across])

    def exists(vertical, across):
        if vertical and across:
            return has[vertical] & has[across]
        return has[vertical or across]

    def opposite(across):
        return {"right": "left", "left": "right", "": ""}[across]

    def remote(number, src, dst, vertical, across):
        return pltpu.make_async_remote_copy(
            src_ref=src, dst_ref=dst, send_sem=ssem.at[number], recv_sem=rsem.at[number],
            device_id=to(vertical, across), device_id_type=MESH,
        )

    sent = {}

    def send(number, src, dst, vertical, across):
        copy = remote(number, src, dst, vertical, across)
        pl.when(exists(vertical, across))(copy.start)
        sent[number] = (copy, vertical, across)

    def arrived(number):
        copy, vertical, across = sent[number]
        pl.when(exists(vertical, opposite(across)))(copy.wait_recv)

    def rows(start):
        return pl.ds(pl.multiple_of(start, 128), 128)

    outer_half, inner_half = rows(128 + 128 * core), rows(256 - 128 * core)
    outer_rim, inner_rim = rows(384 * core), rows(384 - 384 * core)

    local = [
        pltpu.make_async_copy(obj_hbm, obj, lsem.at[0]),
        pltpu.make_async_copy(amp_hbm, amps.at[pl.ds(0, slots)], lsem.at[1]),
        pltpu.make_async_copy(probe_hbm, probe, lsem.at[2]),
        pltpu.make_async_copy(tab_hbm, tab, lsem.at[3]),
    ]
    for copy in local:
        copy.start()

    barrier = pltpu.get_barrier_semaphore()
    for vertical, across in (("", "right"), ("", "left"), ("outer", ""), ("inner", "")):
        pl.when(exists(vertical, across))(
            functools.partial(
                pl.semaphore_signal, barrier, inc=1, device_id=to(vertical, across), device_id_type=MESH
            )
        )

    for c in range(2):
        for b in (0, 3):
            ext[c, b] = jnp.zeros((512, 128), F32)
        for b in (1, 2):
            ext[c, b, 0:128, :] = jnp.zeros((128, 128), F32)
            ext[c, b, 384:512, :] = jnp.zeros((128, 128), F32)
    local[0].wait()
    for c in range(2):
        for b in range(2):
            plane = obj[pl.ds(2 * b + c, 256, stride=4), :]
            ext[c, 1 + b, 128:384, :] = plane
            rim[c, 1 + b, 128:384, :] = plane.astype(BF16)

    neighbours = jnp.int32(1)
    for name in ("right", "left", "outer"):
        neighbours = neighbours + jnp.where(has[name], 1, 0)
    pl.semaphore_wait(barrier, neighbours)

    send(POS, pos, left_pos, "", "right")
    send(CNT, cnt, left_cnt, "", "right")
    for n, half in enumerate((outer_half, inner_half)):
        send(OBJ + 2 * n, rim.at[:, 2, half], rim.at[:, 0, half], "", "right")
        send(OBJ + 2 * n + 1, rim.at[:, 1, half], rim.at[:, 3, half], "", "left")
    send(OBJ + 4, rim.at[:, pl.ds(1, 2), outer_half], rim.at[:, pl.ds(1, 2), inner_rim], "outer", "")
    send(OBJ + 5, rim.at[:, pl.ds(1, 2), inner_half], rim.at[:, pl.ds(1, 2), outer_rim], "inner", "")

    def widen(number, blocks, span):
        copy, vertical, across = sent[number]

        @pl.when(exists(vertical, opposite(across)))
        def _():
            copy.wait_recv()
            for c in range(2):
                for b in blocks:
                    ext[c, b, span, :] = rim[c, b, span, :].astype(F32)

    def corners(n, half, beyond, vertical):
        for m, (side, block) in enumerate((("left", 0), ("right", 3))):
            widen(OBJ + 2 * n + m, [block], half)
            copy = remote(CORNER + 2 * n + m, rim.at[:, block, half], rim.at[:, block, beyond], vertical, "")
            there = exists(vertical, side)
            pl.when(there)(copy.start)
            corner_copies.append((copy, there, block, vertical))

    corner_copies = []

    local[1].wait()
    local[3].wait()

    def reorder(i, carry):
        amps[i] = dot(dot(tab[4], amps[i]).astype(BF16), tab[5]).astype(BF16)
        return carry

    lax.fori_loop(0, slots, reorder, 0)

    def ranked(ref, count, tile):
        rank = jnp.int32(0)
        picked = [[jnp.int32(0)] * 3 for _ in range(4)]
        for i in range(slots):
            y, x = ref[0, 0, i], ref[0, 1, i]
            here = jnp.where((i < count) & ((x >> 8) == tile), 1, 0)
            for j in range(4):
                hit = jnp.where(rank == j, here, 0)
                picked[j] = [old + hit * new for old, new in zip(picked[j], (i, y, x))]
            rank = rank + here
        return picked, rank

    going, _ = ranked(pos, cnt[0, 0], col + 1)
    for j in range(4):
        sa[j] = amps[going[j][0] & (slots - 1)]
    for j in range(4):
        send(AMP + j, sa.at[j], ra.at[j], "", "right")
    corners(0, outer_half, inner_rim, "outer")

    local[2].wait()
    for k in range(modes):
        for c in range(2):
            for b in range(2):
                pp[k, c, b] = probe[pl.ds(k * 1024 + 2 * b + c, 256, stride=4), :]
    for b in range(2):
        for first in range(0, 256, 32):
            total = None
            for k in range(modes):
                for c in range(2):
                    part = pp[k, c, b, first : first + 32, :]
                    total = part * part if total is None else total + part * part
            light[b, first : first + 32, :] = total

    pg[...] = jnp.zeros_like(pg)
    pw[...] = jnp.zeros_like(pw)
    cv[...] = jnp.zeros_like(cv)
    cw[...] = jnp.zeros_like(cw)
    for j in range(4):
        amps[slots + j] = jnp.zeros((256, 256), BF16)

    for side in range(2):

        @pl.when(jnp.logical_not(has[("left", "right")[side]]))
        def _(side=side):
            for ref in (wx, gx):
                ref[:, side] = jnp.zeros(ref.shape[:1] + ref.shape[2:], BF16)

        @pl.when(jnp.logical_not(exists("outer", ("left", "right")[side])))
        def _(side=side):
            for ref in (wd, gd):
                ref[side] = jnp.zeros(ref.shape[1:], BF16)

    @pl.when(jnp.logical_not(has["outer"]))
    def _():
        for ref in (wo, go):
            ref[...] = jnp.zeros(ref.shape, BF16)

    corners(1, inner_half, outer_rim, "inner")

    arrived(POS)
    arrived(CNT)

    @pl.when(jnp.logical_not(has["left"]))
    def _():
        left_cnt[0, 0] = 0
        for i in range(slots):
            for axis in range(2):
                left_pos[0, axis, i] = 0

    home, n_home = ranked(pos, cnt[0, 0], col)
    came, _ = ranked(left_pos, left_cnt[0, 0], col)
    for j in range(4):
        for i in range(2):
            table[3 + i, j] = came[j][1 + i]
    for j in range(4):
        from_left = j >= n_home
        there = jnp.clip(j - n_home, 0, 3)
        table[0, j] = jnp.where(from_left, slots + there, home[j][0])
        for i in range(2):
            table[1 + i, j] = jnp.where(from_left, table[3 + i, there], home[j][1 + i]) & 255

    lanes = lax.broadcasted_iota(jnp.int32, (256, 128), 1)

    def spread(ref, pieces, shift):
        keep = lanes >= shift
        low, high = (pltpu.roll(piece, shift, 1) for piece in pieces)
        ref[1, 256:512, :] = jnp.where(keep, low, 0.0)
        ref[2, 256:512, :] = jnp.where(keep, high, low)
        ref[3, 256:512, :] = jnp.where(keep, 0.0, high)

    def place(canvas, ref, y, block):
        for b in range(4):
            canvas[b] += ref[b - block + 1, pl.ds(256 - y, 512), :]

    def weigh(j, carry):
        y, x = table[1, j], table[2, j]
        spread(pw, [light[0], light[1]], x & 127)
        place(cw.at[0], pw, y, x >> 7)
        return carry

    lax.fori_loop(0, 4, weigh, 0)
    widen(OBJ + 4, [1, 2], outer_rim)
    widen(OBJ + 5, [1, 2], inner_rim)
    for copy, there, block, vertical in corner_copies:
        span = outer_rim if vertical == "outer" else inner_rim

        @pl.when(there)
        def _(copy=copy, block=block, span=span):
            copy.wait_recv()
            for c in range(2):
                ext[c, block, span, :] = rim[c, block, span, :].astype(F32)

    def halo_out(base, canvas, stage, from_inner, from_x, from_corner, from_outer):
        layers = canvas.shape[0]

        def rounded(blocks, span):
            for c in range(layers):
                for b in blocks:
                    stage[c, b, span, :] = canvas[c, b, span, :].astype(BF16)

        rounded(range(4), inner_rim)
        send(base, stage.at[:, :, inner_rim], from_inner, "inner", "")
        rounded((0, 3), outer_half)
        for n, (side, block) in enumerate((("right", 3), ("left", 0))):
            send(base + 1 + n, stage.at[:, block, outer_half], from_x.at[0, n], "", side)
        rounded(range(4), outer_rim)
        for n, (side, block) in enumerate((("right", 3), ("left", 0))):
            send(base + 3 + n, stage.at[:, block, outer_rim], from_corner.at[n], "outer", side)
        send(base + 5, stage.at[:, pl.ds(1, 2), outer_rim], from_outer, "outer", "")

    def halo_inner(base, canvas, stage, from_inner, from_x):
        arrived(base)
        for n, (side, block) in enumerate((("right", 3), ("left", 0))):
            for c in range(canvas.shape[0]):
                total = canvas[c, block, inner_half, :] + from_inner[c, block].astype(F32)
                stage[c, block, inner_half, :] = total.astype(BF16)
            send(base + 6 + n, stage.at[:, block, inner_half], from_x.at[1, n], "", side)

    halo_out(WEIGHT, cw, ws, wi, wx, wd, wo)

    def slot(j, carry):
        y, x = table[1, j], table[2, j]
        block, shift = x >> 7, x & 127
        keep = lanes >= shift
        for c in range(2):
            for b in range(2):
                near = ext[c, block + b, pl.ds(y, 256), :]
                far_off = ext[c, block + b + 1, pl.ds(y, 256), :]
                win[c, b] = pltpu.roll(jnp.where(keep, near, far_off), (128 - shift) & 127, 1)
        for k in range(modes):
            waves = []
            for b in range(2):
                p_re, p_im, w_re, w_im = pp[k, 0, b], pp[k, 1, b], win[0, b], win[1, b]
                waves.append((p_re * w_re - p_im * w_im, p_re * w_im + p_im * w_re))
            (lo_re, lo_im), (hi_re, hi_im) = waves
            even = jnp.concatenate([lo_re + hi_re, lo_im + hi_im], axis=1).astype(BF16)
            odd = jnp.concatenate([lo_re - hi_re, lo_im - hi_im], axis=1).astype(BF16)
            h_even, h_odd = dot(even, tab[0]), dot(odd, tab[1])
            for parity in range(2):
                if parity == 0:
                    e, o = h_even[:128] + h_even[128:], h_odd[:128] + h_odd[128:]
                else:
                    e, o = h_even[:128] - h_even[128:], h_odd[:128] - h_odd[128:]
                stacked = jnp.concatenate(
                    [
                        jnp.concatenate([e[:, :128], o[:, :128]], axis=1),
                        jnp.concatenate([e[:, 128:], o[:, 128:]], axis=1),
                    ],
                    axis=0,
                ).astype(BF16)
                far[parity, k] = dot(tab[2 + parity], stacked)

        @pl.when(has["left"])
        def _():
            remote(AMP + j, sa.at[j], ra.at[j], "", "right").wait_recv()
            amps[slots + j] = ra[j]

        amplitude = amps.at[table[0, j]]
        for parity in range(2):
            intensity = None
            for k in range(modes):
                re, im = far[parity, k, :128, :], far[parity, k, 128:, :]
                term = re * re + im * im
                intensity = term if intensity is None else intensity + term
            held = lax.rsqrt(jnp.maximum(intensity, floor_amplitude * floor_amplitude))
            fac[parity] = 1.0 - amplitude[128 * parity : 128 * parity + 128, :].astype(F32) * held

        for k in range(modes):
            parts = []
            for parity in range(2):
                factor = jnp.concatenate([fac[parity], fac[parity]], axis=0)
                parts.append(dot(tab[parity], (far[parity, k] * factor).astype(BF16)))
            low, high = parts[0] + parts[1], parts[0] - parts[1]
            ends = []
            for parity in range(2):
                cut = slice(128 * parity, 128 * parity + 128)
                near = jnp.concatenate(
                    [
                        jnp.concatenate([low[:128, cut], low[128:, cut]], axis=1),
                        jnp.concatenate([high[:128, cut], high[128:, cut]], axis=1),
                    ],
                    axis=0,
                ).astype(BF16)
                ends.append(dot(near, tab[2 + parity]))
            for b in range(2):
                back = ends[0] + ends[1] if b == 0 else ends[0] - ends[1]
                b_re, b_im = back[:, :128], back[:, 128:]
                p_re, p_im = pp[k, 0, b], pp[k, 1, b]
                g_re, g_im = p_re * b_re + p_im * b_im, p_re * b_im - p_im * b_re
                if k == 0:
                    grad[0, b], grad[1, b] = g_re, g_im
                else:
                    grad[0, b] += g_re
                    grad[1, b] += g_im
        for c in range(2):
            spread(pg.at[c], [grad[c, 0], grad[c, 1]], shift)
            place(cv.at[c], pg.at[c], y, block)
        return carry

    lax.fori_loop(0, 4, slot, 0)

    halo_out(GRAD, cv, gs, gi, gx, gd, go)
    halo_inner(WEIGHT, cw, ws, wi, wx)
    halo_inner(GRAD, cv, gs, gi, gx)

    def whole(canvas, c, b, from_inner, from_x, from_corner, from_outer):
        total = canvas[c, 1 + b, outer_half, :] + from_outer[c, b].astype(F32)
        total = total + from_x[0, b, c].astype(F32) + from_corner[b, c].astype(F32)
        other = canvas[c, 1 + b, inner_half, :] + from_inner[c, 1 + b].astype(F32)
        return total, other + from_x[1, b, c].astype(F32)

    for number in range(1, 8):
        arrived(WEIGHT + number)
    for b in range(2):
        far_half, near_half = whole(cw, 0, b, wi, wx, wd, wo)
        cw[0, 1 + b, outer_half, :] = 1.0 / (far_half + ridge_weight)
        cw[0, 1 + b, inner_half, :] = 1.0 / (near_half + ridge_weight)
    for number in range(1, 8):
        arrived(GRAD + number)
    for c in range(2):
        for b in range(2):
            far_half, near_half = whole(cv, c, b, gi, gx, gd, go)
            first, second = 512 * core + 2 * b + c, 512 - 512 * core + 2 * b + c
            out[pl.ds(first, 128, stride=4), :] = far_half * cw[0, 1 + b, outer_half, :]
            out[pl.ds(second, 128, stride=4), :] = near_half * cw[0, 1 + b, inner_half, :]

    for copy, vertical, across in sent.values():
        pl.when(exists(vertical, across))(copy.wait_send)
    for copy, there, _, _ in corner_copies:
        pl.when(there)(copy.wait_send)


def on_device(n_row, n_col, object_field, probe_modes, amplitudes, positions, counts):
    modes, extent = probe_modes.shape[0], probe_modes.shape[1]
    slots = amplitudes.shape[1]
    half = extent // 2
    obj = object_field.reshape(extent, 2, 2, half).transpose(0, 2, 1, 3).reshape(4 * extent, half)
    probe = probe_modes.reshape(modes, extent, 2, 2, half).transpose(0, 1, 3, 2, 4)
    probe = probe.reshape(modes * 4 * extent, half)
    tab = jnp.asarray(tables(extent))
    big = 2 * extent
    vmem, anywhere = pltpu.VMEM, pl.BlockSpec(memory_space=pl.ANY)
    scratch = [
        vmem((4 * extent, half), F32),
        vmem((modes * 4 * extent, half), F32),
        vmem((slots + 4, extent, extent), BF16),
        vmem((6, extent, extent), BF16),
        vmem((modes, 2, 2, extent, half), F32),
        vmem((2, extent, half), F32),
        vmem((2, 4, big, half), F32),
        vmem((2, 2, extent, half), F32),
        vmem((2, 4, big, half), BF16),
        vmem((4, extent, extent), BF16),
        vmem((4, extent, extent), BF16),
        pltpu.SMEM((1, 2, slots), jnp.int32),
        pltpu.SMEM((1, 1), jnp.int32),
        pltpu.SMEM((5, 4), jnp.int32),
        vmem((2, modes, extent, extent), F32),
        vmem((2, half, extent), F32),
        vmem((2, 2, extent, half), F32),
        vmem((2, 5, 3 * extent, half), F32),
        vmem((5, 3 * extent, half), F32),
        vmem((2, 4, big, half), F32),
        vmem((1, 4, big, half), F32),
        vmem((1, 4, big, half), BF16),
        vmem((1, 4, half, half), BF16),
        vmem((2, 2, 1, half, half), BF16),
        vmem((2, 1, half, half), BF16),
        vmem((1, 2, half, half), BF16),
        vmem((2, 4, big, half), BF16),
        vmem((2, 4, half, half), BF16),
        vmem((2, 2, 2, half, half), BF16),
        vmem((2, 2, half, half), BF16),
        vmem((2, 2, half, half), BF16),
        pltpu.SemaphoreType.DMA((4,)),
        pltpu.SemaphoreType.DMA((COPIES,)),
        pltpu.SemaphoreType.DMA((COPIES,)),
    ]
    update = pl.pallas_call(
        functools.partial(kernel, n_row, n_col, slots, modes),
        out_shape=jax.ShapeDtypeStruct((4 * extent, half), F32),
        in_specs=[anywhere] * 4 + [pl.BlockSpec(memory_space=pltpu.SMEM)] * 2,
        out_specs=pl.BlockSpec(memory_space=pltpu.VMEM),
        scratch_shapes=scratch,
        compiler_params=pltpu.CompilerParams(
            collective_id=0, has_side_effects=True, vmem_limit_bytes=56 * 1024 * 1024
        ),
        cost_estimate=pl.CostEstimate(flops=5 * 10**9, bytes_accessed=5 * 10**6, transcendentals=3 * 10**5),
    )(obj, probe, amplitudes[0], tab, positions.transpose(0, 2, 1), counts)
    return update.reshape(extent, 2, 2, half).transpose(0, 2, 1, 3).reshape(extent, 2, extent)


def solution(mesh):
    in_specs = (
        P("row", None, "col"),
        P(),
        P("row", "col", None, None),
        P("row", "col", None),
        P("row", "col"),
    )
    out_specs = P("row", None, "col")
    step = functools.partial(on_device, mesh.shape["row"], mesh.shape["col"])
    return jax.shard_map(step, mesh=mesh, in_specs=in_specs, out_specs=out_specs, check_vma=False)
```

time: 46.5 us -> 37.4 us (0.80)
  the two profiles are of different devices: /device:TPU:0 before, /device:TPU:15 now
where the time goes in v2:
time: 37.4 us; the launch traced here: 37.2 us
  Pallas kernels  34.5 us (92%)
  local copies, waits for them, and re-layouts  2.01 us (5%)
  between operations  0.66 us (2%)
    pallas_call x1, Pallas kernels, on_device(): pl.pallas_call(functools.partial(kernel, n_row, n_col, slots, modes), out...  34.5 us
    unnamed x1, local copies, waits for them, and re-layouts  2.01 us

profile of v2, /device:TPU:15, one launch (start us, length us, event | category | flops | bytes accessed | tf_op | source)
XLA Modules:
  0.0 37.2 jit_solution(12135929768349269473)
XLA Ops:
  0.7 34.5 %shard_map.64 = f32[1024,128]{1,0:T(8,128)} custom-call(f32[1024,128]{1,0:T(8,128)} %bitcast.20, f32[4096,128]{1,0:T(8,128)} %bitcast.18, bf16[8,256,256]{2,1,0:T(8,128)(2,1)} %bitcast.19, bf16[6,256,256]{2,1,0:T(8,128)(2,1)} %constant.2.clone.tab_hbm, s32[1,2,8]{2,1,0:T(2,128)} %bitcast.21, s32[1,1]{1,0:T(1,128)S(6)} %copy.11.cnt), custom_call_target="tpu_custom_call" | custom-call | flops 5000000000 | bytes 5000000 | tf_op jit(solution)/shard_map/pallas_call | solution.py:472
  35.2 2.0 %copy.12 = f32[256,2,256]{2,1,0:T(2,128)} copy(f32[256,2,256]{2,1,0:T(2,128)} %bitcast.17) | data formatting | bytes 1048576

commit v3 on v2

--- a/solution.py
+++ b/solution.py
@@ -51,7 +51,7 @@
     obj_hbm, probe_hbm, amp_hbm, tab_hbm, pos, cnt, out,
     obj, probe, amps, tab, pp, light, ext, win,
     rim, sa, ra, left_pos, left_cnt, table,
-    far, fac, grad, pg, pw, cv, cw,
+    far, wave, stack, grad, pg, pw, cv, cw,
     ws, wi, wx, wd, wo, gs, gi, gx, gd, go,
     lsem, ssem, rsem,
 ):
@@ -204,9 +204,12 @@
                     total = part * part if total is None else total + part * part
             light[b, first : first + 32, :] = total
 
-    pg[...] = jnp.zeros_like(pg)
+    for c in range(2):
+        pg[c, 12] = jnp.zeros((768, 128), F32)
+        for n in range(12):
+            for first in (0, 512):
+                pg[c, n, first : first + 256, :] = jnp.zeros((256, 128), F32)
     pw[...] = jnp.zeros_like(pw)
-    cv[...] = jnp.zeros_like(cv)
     cw[...] = jnp.zeros_like(cw)
     for j in range(4):
         amps[slots + j] = jnp.zeros((256, 256), BF16)
@@ -283,13 +286,11 @@
             for c in range(2):
                 ext[c, block, span, :] = rim[c, block, span, :].astype(F32)
 
-    def halo_out(base, canvas, stage, from_inner, from_x, from_corner, from_outer):
-        layers = canvas.shape[0]
-
+    def halo_out(base, gather, layers, stage, from_inner, from_x, from_corner, from_outer):
         def rounded(blocks, span):
             for c in range(layers):
                 for b in blocks:
-                    stage[c, b, span, :] = canvas[c, b, span, :].astype(BF16)
+                    stage[c, b, span, :] = gather(c, b, span).astype(BF16)
 
         rounded(range(4), inner_rim)
         send(base, stage.at[:, :, inner_rim], from_inner, "inner", "")
@@ -301,47 +302,142 @@
             send(base + 3 + n, stage.at[:, block, outer_rim], from_corner.at[n], "outer", side)
         send(base + 5, stage.at[:, pl.ds(1, 2), outer_rim], from_outer, "outer", "")
 
-    def halo_inner(base, canvas, stage, from_inner, from_x):
+    def halo_inner(base, gather, layers, stage, from_inner, from_x):
         arrived(base)
         for n, (side, block) in enumerate((("right", 3), ("left", 0))):
-            for c in range(canvas.shape[0]):
-                total = canvas[c, block, inner_half, :] + from_inner[c, block].astype(F32)
+            for c in range(layers):
+                total = gather(c, block, inner_half) + from_inner[c, block].astype(F32)
                 stage[c, block, inner_half, :] = total.astype(BF16)
             send(base + 6 + n, stage.at[:, block, inner_half], from_x.at[1, n], "", side)
 
-    halo_out(WEIGHT, cw, ws, wi, wx, wd, wo)
-
-    def slot(j, carry):
+    def weight_at(c, b, span):
+        return cw[c, b, span, :]
+
+    halo_out(WEIGHT, weight_at, 1, ws, wi, wx, wd, wo)
+
+    def cut_window(j):
         y, x = table[1, j], table[2, j]
         block, shift = x >> 7, x & 127
-        keep = lanes >= shift
+        keep = lax.broadcasted_iota(jnp.int32, (64, 128), 1) >= shift
         for c in range(2):
             for b in range(2):
-                near = ext[c, block + b, pl.ds(y, 256), :]
-                far_off = ext[c, block + b + 1, pl.ds(y, 256), :]
-                win[c, b] = pltpu.roll(jnp.where(keep, near, far_off), (128 - shift) & 127, 1)
+                for first in range(0, 256, 64):
+                    near = ext[c, block + b, pl.ds(y + first, 64), :]
+                    beyond = ext[c, block + b + 1, pl.ds(y + first, 64), :]
+                    win[c, b, first : first + 64, :] = pltpu.roll(
+                        jnp.where(keep, near, beyond), (128 - shift) & 127, 1
+                    )
+
+    group = 4
+
+    def exit_waves():
+        for first in range(0, 256, 16):
+            cut = slice(first, first + 16)
+            at = 2 * first if first < 128 else 2 * (first - 128) + 16
+            w_re = [win[0, b, cut, :] for b in range(2)]
+            w_im = [win[1, b, cut, :] for b in range(2)]
+            for k in range(modes):
+                waves = []
+                for b in range(2):
+                    p_re, p_im = pp[k, 0, b, cut, :], pp[k, 1, b, cut, :]
+                    waves.append((p_re * w_re[b] - p_im * w_im[b], p_re * w_im[b] + p_im * w_re[b]))
+                to_rows = slice(256 * k + at, 256 * k + at + 16)
+                for part in range(2):
+                    low, high = waves[0][part], waves[1][part]
+                    lanes_of = slice(128 * part, 128 * part + 128)
+                    wave[0, to_rows, lanes_of] = (low + high).astype(BF16)
+                    wave[1, to_rows, lanes_of] = (low - high).astype(BF16)
+
+    def half_done():
+        for parity in range(2):
+            lanes_of = slice(128 * parity, 128 * parity + 128)
+            for k in range(0, modes, group):
+                done = dot(wave[parity, 256 * k : 256 * (k + group), :], tab[parity])
+                for m in range(group):
+                    for first in range(0, 128, 16):
+                        at = 256 * m + 2 * first
+                        low, high = done[at : at + 16], done[at + 16 : at + 32]
+                        plus, minus = (low + high).astype(BF16), (low - high).astype(BF16)
+                        for part in range(2):
+                            to_rows = slice(128 * part + first, 128 * part + first + 16)
+                            source = slice(128 * part, 128 * part + 128)
+                            stack[0, k + m, to_rows, lanes_of] = plus[:, source]
+                            stack[1, k + m, to_rows, lanes_of] = minus[:, source]
+
+    def far_field():
+        for parity in range(2):
+            for k in range(modes):
+                far[parity, k] = dot(tab[2 + parity], stack[parity, k])
+
+    def residue(parity, amplitude):
+        for first in range(0, 128, 16):
+            upper, lower = slice(first, first + 16), slice(128 + first, 144 + first)
+            re = [far[parity, k, upper, :] for k in range(modes)]
+            im = [far[parity, k, lower, :] for k in range(modes)]
+            intensity = None
+            for k in range(modes):
+                term = re[k] * re[k] + im[k] * im[k]
+                intensity = term if intensity is None else intensity + term
+            held = lax.rsqrt(jnp.maximum(intensity, floor_amplitude * floor_amplitude))
+            measured = amplitude[128 * parity + first : 128 * parity + first + 16, :].astype(F32)
+            factor = 1.0 - measured * held
+            for k in range(modes):
+                stack[parity, k, upper, :] = (re[k] * factor).astype(BF16)
+                stack[parity, k, lower, :] = (im[k] * factor).astype(BF16)
+
+    def near_field():
         for k in range(modes):
-            waves = []
+            even, odd = dot(tab[0], stack[0, k]), dot(tab[1], stack[1, k])
+            for first in range(0, 256, 16):
+                cut = slice(first, first + 16)
+                part, at = first // 128, 256 * k + first % 128
+                lanes_of = slice(128 * part, 128 * part + 128)
+                plus, minus = (even[cut] + odd[cut]).astype(BF16), (even[cut] - odd[cut]).astype(BF16)
+                for column in range(2):
+                    source = slice(128 * column, 128 * column + 128)
+                    wave[column, at : at + 16, lanes_of] = plus[:, source]
+                    wave[column, 128 + at : 144 + at, lanes_of] = minus[:, source]
+
+    def back_parts():
+        for parity in range(2):
+            for k in range(0, modes, group):
+                back = dot(wave[parity, 256 * k : 256 * (k + group), :], tab[2 + parity])
+                for m in range(group):
+                    far[parity, k + m] = back[256 * m : 256 * m + 256]
+
+    def gradient():
+        for first in range(0, 256, 16):
+            cut = slice(first, first + 16)
+            total = [None] * 4
+            for k in range(modes):
+                e_re, o_re = far[0, k, cut, 0:128], far[1, k, cut, 0:128]
+                e_im, o_im = far[0, k, cut, 128:256], far[1, k, cut, 128:256]
+                for b in range(2):
+                    b_re = e_re + o_re if b == 0 else e_re - o_re
+                    b_im = e_im + o_im if b == 0 else e_im - o_im
+                    p_re, p_im = pp[k, 0, b, cut, :], pp[k, 1, b, cut, :]
+                    for n, term in ((b, p_re * b_re + p_im * b_im), (2 + b, p_re * b_im - p_im * b_re)):
+                        total[n] = term if total[n] is None else total[n] + term
             for b in range(2):
-                p_re, p_im, w_re, w_im = pp[k, 0, b], pp[k, 1, b], win[0, b], win[1, b]
-                waves.append((p_re * w_re - p_im * w_im, p_re * w_im + p_im * w_re))
-            (lo_re, lo_im), (hi_re, hi_im) = waves
-            even = jnp.concatenate([lo_re + hi_re, lo_im + hi_im], axis=1).astype(BF16)
-            odd = jnp.concatenate([lo_re - hi_re, lo_im - hi_im], axis=1).astype(BF16)
-            h_even, h_odd = dot(even, tab[0]), dot(odd, tab[1])
-            for parity in range(2):
-                if parity == 0:
-                    e, o = h_even[:128] + h_even[128:], h_odd[:128] + h_odd[128:]
-                else:
-                    e, o = h_even[:128] - h_even[128:], h_odd[:128] - h_odd[128:]
-                stacked = jnp.concatenate(
-                    [
-                        jnp.concatenate([e[:, :128], o[:, :128]], axis=1),
-                        jnp.concatenate([e[:, 128:], o[:, 128:]], axis=1),
-                    ],
-                    axis=0,
-                ).astype(BF16)
-                far[parity, k] = dot(tab[2 + parity], stacked)
+                grad[0, b, cut, :] = total[b]
+                grad[1, b, cut, :] = total[2 + b]
+
+    def keep_gradient(j):
+        shift = table[2, j] & 127
+        for first in range(0, 256, 64):
+            cut, at = slice(first, first + 64), slice(256 + first, 320 + first)
+            keep = lax.broadcasted_iota(jnp.int32, (64, 128), 1) >= shift
+            for c in range(2):
+                low, high = (pltpu.roll(grad[c, b, cut, :], shift, 1) for b in range(2))
+                pg[c, 3 * j, at, :] = jnp.where(keep, low, 0.0)
+                pg[c, 3 * j + 1, at, :] = jnp.where(keep, high, low)
+                pg[c, 3 * j + 2, at, :] = jnp.where(keep, 0.0, high)
+
+    def slot(j, carry):
+        cut_window(j)
+        exit_waves()
+        half_done()
+        far_field()
 
         @pl.when(has["left"])
         def _():
@@ -350,69 +446,53 @@
 
         amplitude = amps.at[table[0, j]]
         for parity in range(2):
-            intensity = None
-            for k in range(modes):
-                re, im = far[parity, k, :128, :], far[parity, k, 128:, :]
-                term = re * re + im * im
-                intensity = term if intensity is None else intensity + term
-            held = lax.rsqrt(jnp.maximum(intensity, floor_amplitude * floor_amplitude))
-            fac[parity] = 1.0 - amplitude[128 * parity : 128 * parity + 128, :].astype(F32) * held
-
-        for k in range(modes):
-            parts = []
-            for parity in range(2):
-                factor = jnp.concatenate([fac[parity], fac[parity]], axis=0)
-                parts.append(dot(tab[parity], (far[parity, k] * factor).astype(BF16)))
-            low, high = parts[0] + parts[1], parts[0] - parts[1]
-            ends = []
-            for parity in range(2):
-                cut = slice(128 * parity, 128 * parity + 128)
-                near = jnp.concatenate(
-                    [
-                        jnp.concatenate([low[:128, cut], low[128:, cut]], axis=1),
-                        jnp.concatenate([high[:128, cut], high[128:, cut]], axis=1),
-                    ],
-                    axis=0,
-                ).astype(BF16)
-                ends.append(dot(near, tab[2 + parity]))
-            for b in range(2):
-                back = ends[0] + ends[1] if b == 0 else ends[0] - ends[1]
-                b_re, b_im = back[:, :128], back[:, 128:]
-                p_re, p_im = pp[k, 0, b], pp[k, 1, b]
-                g_re, g_im = p_re * b_re + p_im * b_im, p_re * b_im - p_im * b_re
-                if k == 0:
-                    grad[0, b], grad[1, b] = g_re, g_im
-                else:
-                    grad[0, b] += g_re
-                    grad[1, b] += g_im
-        for c in range(2):
-            spread(pg.at[c], [grad[c, 0], grad[c, 1]], shift)
-            place(cv.at[c], pg.at[c], y, block)
+            residue(parity, amplitude)
+        near_field()
+        back_parts()
+        gradient()
+        keep_gradient(j)
         return carry
 
     lax.fori_loop(0, 4, slot, 0)
 
-    halo_out(GRAD, cv, gs, gi, gx, gd, go)
-    halo_inner(WEIGHT, cw, ws, wi, wx)
-    halo_inner(GRAD, cv, gs, gi, gx)
-
-    def whole(canvas, c, b, from_inner, from_x, from_corner, from_outer):
-        total = canvas[c, 1 + b, outer_half, :] + from_outer[c, b].astype(F32)
+    def gradient_at(c, b, span):
+        total = None
+        for j in range(4):
+            y, block = table[1, j], table[2, j] >> 7
+            inside = (b >= block) & (b < block + 3)
+            part = pg[c, jnp.where(inside, 3 * j + b - block, 12), pl.ds(256 - y + span.start, 128), :]
+            total = part if total is None else total + part
+        return total
+
+    halo_out(GRAD, gradient_at, 2, gs, gi, gx, gd, go)
+    halo_inner(WEIGHT, weight_at, 1, ws, wi, wx)
+    halo_inner(GRAD, gradient_at, 2, gs, gi, gx)
+
+    def whole(gather, c, b, from_inner, from_x, from_corner, from_outer):
+        total = gather(c, 1 + b, outer_half) + from_outer[c, b].astype(F32)
         total = total + from_x[0, b, c].astype(F32) + from_corner[b, c].astype(F32)
-        other = canvas[c, 1 + b, inner_half, :] + from_inner[c, 1 + b].astype(F32)
+        other = gather(c, 1 + b, inner_half) + from_inner[c, 1 + b].astype(F32)
         return total, other + from_x[1, b, c].astype(F32)
+
+    for c in range(2):
+        for b in (1, 2):
+            for span in (outer_half, inner_half):
+                cv[c, b, span, :] = gradient_at(c, b, span)
+
+    def own_gradient(c, b, span):
+        return cv[c, b, span, :]
 
     for number in range(1, 8):
         arrived(WEIGHT + number)
     for b in range(2):
-        far_half, near_half = whole(cw, 0, b, wi, wx, wd, wo)
+        far_half, near_half = whole(weight_at, 0, b, wi, wx, wd, wo)
         cw[0, 1 + b, outer_half, :] = 1.0 / (far_half + ridge_weight)
         cw[0, 1 + b, inner_half, :] = 1.0 / (near_half + ridge_weight)
     for number in range(1, 8):
         arrived(GRAD + number)
     for c in range(2):
         for b in range(2):
-            far_half, near_half = whole(cv, c, b, gi, gx, gd, go)
+            far_half, near_half = whole(own_gradient, c, b, gi, gx, gd, go)
             first, second = 512 * core + 2 * b + c, 512 - 512 * core + 2 * b + c
             out[pl.ds(first, 128, stride=4), :] = far_half * cw[0, 1 + b, outer_half, :]
             out[pl.ds(second, 128, stride=4), :] = near_half * cw[0, 1 + b, inner_half, :]
@@ -449,9 +529,10 @@
         pltpu.SMEM((1, 1), jnp.int32),
         pltpu.SMEM((5, 4), jnp.int32),
         vmem((2, modes, extent, extent), F32),
-        vmem((2, half, extent), F32),
+        vmem((2, modes * extent, extent), BF16),
+        vmem((2, modes, extent, extent), BF16),
         vmem((2, 2, extent, half), F32),
-        vmem((2, 5, 3 * extent, half), F32),
+        vmem((2, 13, 3 * extent, half), F32),
         vmem((5, 3 * extent, half), F32),
         vmem((2, 4, big, half), F32),
         vmem((1, 4, big, half), F32),

time: 37.4 us -> 34.7 us (0.928)
  the two profiles are of different devices: /device:TPU:15 before, /device:TPU:78 now
where the time goes in v3:
time: 34.7 us; the launch traced here: 34.5 us
  Pallas kernels  31.8 us (92%)
  local copies, waits for them, and re-layouts  2.01 us (6%)
  between operations  0.66 us (2%)
    pallas_call x1, Pallas kernels, on_device(): pl.pallas_call(functools.partial(kernel, n_row, n_col, slots, modes), out...  31.8 us
    unnamed x1, local copies, waits for them, and re-layouts  2.01 us

profile of v3, /device:TPU:78, one launch (start us, length us, event | category | flops | bytes accessed | tf_op | source)
XLA Modules:
  0.0 34.5 jit_solution(3395863479891544202)
XLA Ops:
  0.7 31.8 %shard_map.64 = f32[1024,128]{1,0:T(8,128)} custom-call(f32[1024,128]{1,0:T(8,128)} %bitcast.20, f32[4096,128]{1,0:T(8,128)} %bitcast.18, bf16[8,256,256]{2,1,0:T(8,128)(2,1)} %bitcast.19, bf16[6,256,256]{2,1,0:T(8,128)(2,1)} %constant.2.clone.tab_hbm, s32[1,2,8]{2,1,0:T(2,128)} %bitcast.21, s32[1,1]{1,0:T(1,128)S(6)} %copy.11.cnt), custom_call_target="tpu_custom_call" | custom-call | flops 5000000000 | bytes 5000000 | tf_op jit(solution)/shard_map/pallas_call | solution.py:553
  32.5 2.0 %copy.12 = f32[256,2,256]{2,1,0:T(2,128)} copy(f32[256,2,256]{2,1,0:T(2,128)} %bitcast.17) | data formatting | bytes 1048576

commit v4 on v3

--- a/solution.py
+++ b/solution.py
@@ -48,10 +48,10 @@
 
 def kernel(
     n_row, n_col, slots, modes,
-    obj_hbm, probe_hbm, amp_hbm, tab_hbm, pos, cnt, out,
-    obj, probe, amps, tab, pp, light, ext, win,
+    obj_hbm, probe_hbm, amp_hbm, tab_hbm, pos_hbm, cnt_hbm, out,
+    pos, cnt, obj, probe, amps, tab, pp, light, ext, win,
     rim, sa, ra, left_pos, left_cnt, table,
-    far, wave, stack, grad, pg, pw, cv, cw,
+    far, ends, wave, near, stack, turned, grad, pg, pw, cv, cw,
     ws, wi, wx, wd, wo, gs, gi, gx, gd, go,
     lsem, ssem, rsem,
 ):
@@ -104,9 +104,11 @@
         pltpu.make_async_copy(amp_hbm, amps.at[pl.ds(0, slots)], lsem.at[1]),
         pltpu.make_async_copy(probe_hbm, probe, lsem.at[2]),
         pltpu.make_async_copy(tab_hbm, tab, lsem.at[3]),
+        pltpu.make_async_copy(pos_hbm, pos, lsem.at[4]),
+        pltpu.make_async_copy(cnt_hbm, cnt, lsem.at[5]),
     ]
-    for copy in local:
-        copy.start()
+    for n in (0, 4, 5):
+        local[n].start()
 
     barrier = pltpu.get_barrier_semaphore()
     for vertical, across in (("", "right"), ("", "left"), ("outer", ""), ("inner", "")):
@@ -123,6 +125,8 @@
             ext[c, b, 0:128, :] = jnp.zeros((128, 128), F32)
             ext[c, b, 384:512, :] = jnp.zeros((128, 128), F32)
     local[0].wait()
+    for n in (1, 3, 2):
+        local[n].start()
     for c in range(2):
         for b in range(2):
             plane = obj[pl.ds(2 * b + c, 256, stride=4), :]
@@ -134,6 +138,8 @@
         neighbours = neighbours + jnp.where(has[name], 1, 0)
     pl.semaphore_wait(barrier, neighbours)
 
+    local[4].wait()
+    local[5].wait()
     send(POS, pos, left_pos, "", "right")
     send(CNT, cnt, left_cnt, "", "right")
     for n, half in enumerate((outer_half, inner_half)):
@@ -328,46 +334,52 @@
                         jnp.where(keep, near, beyond), (128 - shift) & 127, 1
                     )
 
-    group = 4
 
     def exit_waves():
-        for first in range(0, 256, 16):
+        def piece(first, k):
             cut = slice(first, first + 16)
             at = 2 * first if first < 128 else 2 * (first - 128) + 16
-            w_re = [win[0, b, cut, :] for b in range(2)]
-            w_im = [win[1, b, cut, :] for b in range(2)]
-            for k in range(modes):
-                waves = []
-                for b in range(2):
-                    p_re, p_im = pp[k, 0, b, cut, :], pp[k, 1, b, cut, :]
-                    waves.append((p_re * w_re[b] - p_im * w_im[b], p_re * w_im[b] + p_im * w_re[b]))
-                to_rows = slice(256 * k + at, 256 * k + at + 16)
-                for part in range(2):
-                    low, high = waves[0][part], waves[1][part]
-                    lanes_of = slice(128 * part, 128 * part + 128)
-                    wave[0, to_rows, lanes_of] = (low + high).astype(BF16)
-                    wave[1, to_rows, lanes_of] = (low - high).astype(BF16)
+            waves = []
+            for b in range(2):
+                p_re, p_im, w_re, w_im = pp[k, 0, b, cut, :], pp[k, 1, b, cut, :], win[0, b, cut, :], win[1, b, cut, :]
+                waves.append((p_re * w_re - p_im * w_im, p_re * w_im + p_im * w_re))
+            to_rows = slice(256 * k + at, 256 * k + at + 16)
+            for part in range(2):
+                low, high = waves[0][part], waves[1][part]
+                lanes_of = slice(128 * part, 128 * part + 128)
+                wave[0, to_rows, lanes_of] = (low + high).astype(BF16)
+                wave[1, to_rows, lanes_of] = (low - high).astype(BF16)
+
+        return [functools.partial(piece, first, k) for first in range(0, 256, 16) for k in range(modes)]
 
     def half_done():
+        done = {}
+
+        def product(parity):
+            done[parity] = dot(wave[parity], tab[parity])
+
+        def piece(parity, k, first):
+            lanes_of = slice(128 * parity, 128 * parity + 128)
+            at = 256 * k + 2 * first
+            low, high = done[parity][at : at + 16], done[parity][at + 16 : at + 32]
+            plus, minus = (low + high).astype(BF16), (low - high).astype(BF16)
+            for part in range(2):
+                to_rows = slice(128 * part + first, 128 * part + first + 16)
+                source = slice(128 * part, 128 * part + 128)
+                stack[0, k, to_rows, lanes_of] = plus[:, source]
+                stack[1, k, to_rows, lanes_of] = minus[:, source]
+
+        pieces = []
         for parity in range(2):
-            lanes_of = slice(128 * parity, 128 * parity + 128)
-            for k in range(0, modes, group):
-                done = dot(wave[parity, 256 * k : 256 * (k + group), :], tab[parity])
-                for m in range(group):
-                    for first in range(0, 128, 16):
-                        at = 256 * m + 2 * first
-                        low, high = done[at : at + 16], done[at + 16 : at + 32]
-                        plus, minus = (low + high).astype(BF16), (low - high).astype(BF16)
-                        for part in range(2):
-                            to_rows = slice(128 * part + first, 128 * part + first + 16)
-                            source = slice(128 * part, 128 * part + 128)
-                            stack[0, k + m, to_rows, lanes_of] = plus[:, source]
-                            stack[1, k + m, to_rows, lanes_of] = minus[:, source]
+            pieces.append(functools.partial(product, parity))
+            pieces += [functools.partial(piece, parity, k, f) for k in range(modes) for f in range(0, 128, 16)]
+        return pieces
 
     def far_field():
-        for parity in range(2):
-            for k in range(modes):
-                far[parity, k] = dot(tab[2 + parity], stack[parity, k])
+        def piece(parity, k):
+            far[parity, k] = dot(tab[2 + parity], stack[parity, k])
+
+        return [functools.partial(piece, parity, k) for parity in range(2) for k in range(modes)]
 
     def residue(parity, amplitude):
         for first in range(0, 128, 16):
@@ -382,36 +394,47 @@
             measured = amplitude[128 * parity + first : 128 * parity + first + 16, :].astype(F32)
             factor = 1.0 - measured * held
             for k in range(modes):
-                stack[parity, k, upper, :] = (re[k] * factor).astype(BF16)
-                stack[parity, k, lower, :] = (im[k] * factor).astype(BF16)
+                turned[parity, k, upper, :] = (re[k] * factor).astype(BF16)
+                turned[parity, k, lower, :] = (im[k] * factor).astype(BF16)
 
     def near_field():
+        done = {}
+
+        def product(parity, k):
+            done[parity, k] = dot(tab[parity], turned[parity, k])
+
+        def piece(k, first):
+            cut = slice(first, first + 16)
+            part, at = first // 128, 256 * k + first % 128
+            lanes_of = slice(128 * part, 128 * part + 128)
+            even, odd = done[0, k][cut], done[1, k][cut]
+            plus, minus = (even + odd).astype(BF16), (even - odd).astype(BF16)
+            for column in range(2):
+                source = slice(128 * column, 128 * column + 128)
+                near[column, at : at + 16, lanes_of] = plus[:, source]
+                near[column, 128 + at : 144 + at, lanes_of] = minus[:, source]
+
+        pieces = []
         for k in range(modes):
-            even, odd = dot(tab[0], stack[0, k]), dot(tab[1], stack[1, k])
-            for first in range(0, 256, 16):
-                cut = slice(first, first + 16)
-                part, at = first // 128, 256 * k + first % 128
-                lanes_of = slice(128 * part, 128 * part + 128)
-                plus, minus = (even[cut] + odd[cut]).astype(BF16), (even[cut] - odd[cut]).astype(BF16)
-                for column in range(2):
-                    source = slice(128 * column, 128 * column + 128)
-                    wave[column, at : at + 16, lanes_of] = plus[:, source]
-                    wave[column, 128 + at : 144 + at, lanes_of] = minus[:, source]
+            pieces += [functools.partial(product, parity, k) for parity in range(2)]
+            pieces += [functools.partial(piece, k, first) for first in range(0, 256, 16)]
+        return pieces
 
     def back_parts():
-        for parity in range(2):
-            for k in range(0, modes, group):
-                back = dot(wave[parity, 256 * k : 256 * (k + group), :], tab[2 + parity])
-                for m in range(group):
-                    far[parity, k + m] = back[256 * m : 256 * m + 256]
+        def piece(parity):
+            back = dot(near[parity], tab[2 + parity])
+            for k in range(modes):
+                ends[parity, k] = back[256 * k : 256 * k + 256]
+
+        return [functools.partial(piece, parity) for parity in range(2)]
 
     def gradient():
-        for first in range(0, 256, 16):
+        def piece(first):
             cut = slice(first, first + 16)
             total = [None] * 4
             for k in range(modes):
-                e_re, o_re = far[0, k, cut, 0:128], far[1, k, cut, 0:128]
-                e_im, o_im = far[0, k, cut, 128:256], far[1, k, cut, 128:256]
+                e_re, o_re = ends[0, k, cut, 0:128], ends[1, k, cut, 0:128]
+                e_im, o_im = ends[0, k, cut, 128:256], ends[1, k, cut, 128:256]
                 for b in range(2):
                     b_re = e_re + o_re if b == 0 else e_re - o_re
                     b_im = e_im + o_im if b == 0 else e_im - o_im
@@ -421,6 +444,13 @@
             for b in range(2):
                 grad[0, b, cut, :] = total[b]
                 grad[1, b, cut, :] = total[2 + b]
+
+        return [functools.partial(piece, first) for first in range(0, 256, 16)]
+
+    def take_turns(*stages):
+        marked = [((n + 0.5) / len(stage), m, piece) for m, stage in enumerate(stages) for n, piece in enumerate(stage)]
+        for _, _, piece in sorted(marked, key=lambda entry: entry[:2]):
+            piece()
 
     def keep_gradient(j):
         shift = table[2, j] & 127
@@ -433,12 +463,13 @@
                 pg[c, 3 * j + 1, at, :] = jnp.where(keep, high, low)
                 pg[c, 3 * j + 2, at, :] = jnp.where(keep, 0.0, high)
 
-    def slot(j, carry):
+    def start_window(j):
         cut_window(j)
-        exit_waves()
-        half_done()
-        far_field()
-
+        take_turns(exit_waves())
+        take_turns(half_done())
+        take_turns(far_field())
+
+    def factor_window(j):
         @pl.when(has["left"])
         def _():
             remote(AMP + j, sa.at[j], ra.at[j], "", "right").wait_recv()
@@ -447,13 +478,23 @@
         amplitude = amps.at[table[0, j]]
         for parity in range(2):
             residue(parity, amplitude)
-        near_field()
-        back_parts()
-        gradient()
+
+    def slot(j, carry):
+        factor_window(j)
+        cut_window(j + 1)
+        take_turns(near_field(), exit_waves())
+        take_turns(half_done())
+        take_turns(back_parts())
+        take_turns(far_field(), gradient())
         keep_gradient(j)
         return carry
 
-    lax.fori_loop(0, 4, slot, 0)
+    start_window(0)
+    lax.fori_loop(0, 3, slot, 0)
+    factor_window(3)
+    for stage in (near_field, back_parts, gradient):
+        take_turns(stage())
+    keep_gradient(3)
 
     def gradient_at(c, b, span):
         total = None
@@ -514,6 +555,8 @@
     big = 2 * extent
     vmem, anywhere = pltpu.VMEM, pl.BlockSpec(memory_space=pl.ANY)
     scratch = [
+        pltpu.SMEM((1, 2, slots), jnp.int32),
+        pltpu.SMEM((1, 1), jnp.int32),
         vmem((4 * extent, half), F32),
         vmem((modes * 4 * extent, half), F32),
         vmem((slots + 4, extent, extent), BF16),
@@ -529,7 +572,10 @@
         pltpu.SMEM((1, 1), jnp.int32),
         pltpu.SMEM((5, 4), jnp.int32),
         vmem((2, modes, extent, extent), F32),
+        vmem((2, modes, extent, extent), F32),
         vmem((2, modes * extent, extent), BF16),
+        vmem((2, modes * extent, extent), BF16),
+        vmem((2, modes, extent, extent), BF16),
         vmem((2, modes, extent, extent), BF16),
         vmem((2, 2, extent, half), F32),
         vmem((2, 13, 3 * extent, half), F32),
@@ -546,14 +592,14 @@
         vmem((2, 2, 2, half, half), BF16),
         vmem((2, 2, half, half), BF16),
         vmem((2, 2, half, half), BF16),
-        pltpu.SemaphoreType.DMA((4,)),
+        pltpu.SemaphoreType.DMA((6,)),
         pltpu.SemaphoreType.DMA((COPIES,)),
         pltpu.SemaphoreType.DMA((COPIES,)),
     ]
     update = pl.pallas_call(
         functools.partial(kernel, n_row, n_col, slots, modes),
-        out_shape=jax.ShapeDtypeStruct((4 * extent, half), F32),
-        in_specs=[anywhere] * 4 + [pl.BlockSpec(memory_space=pltpu.SMEM)] * 2,
+        out_shape=pltpu.VMEM((4 * extent, half), F32),
+        in_specs=[anywhere] * 6,
         out_specs=pl.BlockSpec(memory_space=pltpu.VMEM),
         scratch_shapes=scratch,
         compiler_params=pltpu.CompilerParams(

time: 34.7 us -> 31.2 us (0.90)
  the two profiles are of different devices: /device:TPU:78 before, /device:TPU:15 now
where the time goes in v4:
time: 31.2 us; the launch traced here: 30.6 us
  Pallas kernels  29.2 us (94%)
  local copies, waits for them, and re-layouts  0.8 us (3%)
  between operations  0.66 us (2%)
    pallas_call x1, Pallas kernels, on_device(): pl.pallas_call(functools.partial(kernel, n_row, n_col, slots, modes), out...  29.2 us
    unnamed x1, local copies, waits for them, and re-layouts  0.8 us

profile of v4, /device:TPU:15, one launch (start us, length us, event | category | flops | bytes accessed | tf_op | source)
XLA Modules:
  0.0 30.6 jit_solution(14859457026895646273)
XLA Ops:
  0.7 29.2 %shard_map.64 = f32[1024,128]{1,0:T(8,128)S(1)} custom-call(f32[1024,128]{1,0:T(8,128)} %bitcast.20, f32[4096,128]{1,0:T(8,128)} %bitcast.18, bf16[8,256,256]{2,1,0:T(8,128)(2,1)} %bitcast.19, bf16[6,256,256]{2,1,0:T(8,128)(2,1)} %constant.2.clone.tab_hbm, s32[1,2,8]{2,1,0:T(2,128)} %bitcast.21, s32[1,1]{1,0:T(1,128)S(6)} %copy.12.cnt_hbm), custom_call_target="tpu_custom_call" | custom-call | flops 5000000000 | bytes 5000000 | tf_op jit(solution)/shard_map/pallas_call | solution.py:599
  29.8 0.8 %copy.11 = f32[256,2,256]{2,1,0:T(2,128)} copy(f32[256,2,256]{2,1,0:T(2,128)S(1)} %bitcast.17) | data formatting | bytes 1048576

commit v5 on v4

--- a/solution.py
+++ b/solution.py
@@ -49,7 +49,7 @@
 def kernel(
     n_row, n_col, slots, modes,
     obj_hbm, probe_hbm, amp_hbm, tab_hbm, pos_hbm, cnt_hbm, out,
-    pos, cnt, obj, probe, amps, tab, pp, light, ext, win,
+    pos, cnt, obj, probe, amps, held, tab, pp, light, ext, win,
     rim, sa, ra, left_pos, left_cnt, table,
     far, ends, wave, near, stack, turned, grad, pg, pw, cv, cw,
     ws, wi, wx, wd, wo, gs, gi, gx, gd, go,
@@ -101,7 +101,7 @@
 
     local = [
         pltpu.make_async_copy(obj_hbm, obj, lsem.at[0]),
-        pltpu.make_async_copy(amp_hbm, amps.at[pl.ds(0, slots)], lsem.at[1]),
+        pltpu.make_async_copy(amp_hbm, amps, lsem.at[1]),
         pltpu.make_async_copy(probe_hbm, probe, lsem.at[2]),
         pltpu.make_async_copy(tab_hbm, tab, lsem.at[3]),
         pltpu.make_async_copy(pos_hbm, pos, lsem.at[4]),
@@ -168,15 +168,6 @@
 
     corner_copies = []
 
-    local[1].wait()
-    local[3].wait()
-
-    def reorder(i, carry):
-        amps[i] = dot(dot(tab[4], amps[i]).astype(BF16), tab[5]).astype(BF16)
-        return carry
-
-    lax.fori_loop(0, slots, reorder, 0)
-
     def ranked(ref, count, tile):
         rank = jnp.int32(0)
         picked = [[jnp.int32(0)] * 3 for _ in range(4)]
@@ -189,11 +180,19 @@
             rank = rank + here
         return picked, rank
 
+    def reorder(picked, there):
+        halves = [dot(tab[4], amps[picked[j][0] & (slots - 1)]).astype(BF16) for j in range(4)]
+        for j in range(4):
+            there[j] = dot(halves[j], tab[5]).astype(BF16)
+
     going, _ = ranked(pos, cnt[0, 0], col + 1)
-    for j in range(4):
-        sa[j] = amps[going[j][0] & (slots - 1)]
-    for j in range(4):
+    local[1].wait()
+    local[3].wait()
+    reorder(going, sa)
+    for j in range(1):
         send(AMP + j, sa.at[j], ra.at[j], "", "right")
+    home, n_home = ranked(pos, cnt[0, 0], col)
+    reorder(home, held)
     corners(0, outer_half, inner_rim, "outer")
 
     local[2].wait()
@@ -218,7 +217,7 @@
     pw[...] = jnp.zeros_like(pw)
     cw[...] = jnp.zeros_like(cw)
     for j in range(4):
-        amps[slots + j] = jnp.zeros((256, 256), BF16)
+        held[4 + j] = jnp.zeros((256, 256), BF16)
 
     for side in range(2):
 
@@ -238,6 +237,8 @@
             ref[...] = jnp.zeros(ref.shape, BF16)
 
     corners(1, inner_half, outer_rim, "inner")
+    for j in range(1, 4):
+        send(AMP + j, sa.at[j], ra.at[j], "", "right")
 
     arrived(POS)
     arrived(CNT)
@@ -249,7 +250,6 @@
             for axis in range(2):
                 left_pos[0, axis, i] = 0
 
-    home, n_home = ranked(pos, cnt[0, 0], col)
     came, _ = ranked(left_pos, left_cnt[0, 0], col)
     for j in range(4):
         for i in range(2):
@@ -257,7 +257,7 @@
     for j in range(4):
         from_left = j >= n_home
         there = jnp.clip(j - n_home, 0, 3)
-        table[0, j] = jnp.where(from_left, slots + there, home[j][0])
+        table[0, j] = jnp.where(from_left, 4 + there, j)
         for i in range(2):
             table[1 + i, j] = jnp.where(from_left, table[3 + i, there], home[j][1 + i]) & 255
 
@@ -473,9 +473,9 @@
         @pl.when(has["left"])
         def _():
             remote(AMP + j, sa.at[j], ra.at[j], "", "right").wait_recv()
-            amps[slots + j] = ra[j]
-
-        amplitude = amps.at[table[0, j]]
+            held[4 + j] = ra[j]
+
+        amplitude = held.at[table[0, j]]
         for parity in range(2):
             residue(parity, amplitude)
 
@@ -491,6 +491,7 @@
 
     start_window(0)
     lax.fori_loop(0, 3, slot, 0)
+    halo_inner(WEIGHT, weight_at, 1, ws, wi, wx)
     factor_window(3)
     for stage in (near_field, back_parts, gradient):
         take_turns(stage())
@@ -506,7 +507,6 @@
         return total
 
     halo_out(GRAD, gradient_at, 2, gs, gi, gx, gd, go)
-    halo_inner(WEIGHT, weight_at, 1, ws, wi, wx)
     halo_inner(GRAD, gradient_at, 2, gs, gi, gx)
 
     def whole(gather, c, b, from_inner, from_x, from_corner, from_outer):
@@ -559,7 +559,8 @@
         pltpu.SMEM((1, 1), jnp.int32),
         vmem((4 * extent, half), F32),
         vmem((modes * 4 * extent, half), F32),
-        vmem((slots + 4, extent, extent), BF16),
+        vmem((slots, extent, extent), BF16),
+        vmem((8, extent, extent), BF16),
         vmem((6, extent, extent), BF16),
         vmem((modes, 2, 2, extent, half), F32),
         vmem((2, extent, half), F32),

time: 31.2 us -> 30.8 us (0.987)
  no operation moved by 1% of the time
where the time goes in v5:
time: 30.8 us; the launch traced here: 30.3 us
  Pallas kernels  28.9 us (94%)
  local copies, waits for them, and re-layouts  0.8 us (3%)
  between operations  0.66 us (2%)
    pallas_call x1, Pallas kernels, on_device(): pl.pallas_call(functools.partial(kernel, n_row, n_col, slots, modes), out...  28.9 us
    unnamed x1, local copies, waits for them, and re-layouts  0.8 us

profile of v5, /device:TPU:15, one launch (start us, length us, event | category | flops | bytes accessed | tf_op | source)
XLA Modules:
  0.0 30.3 jit_solution(11489475220641260706)
XLA Ops:
  0.7 28.9 %shard_map.64 = f32[1024,128]{1,0:T(8,128)S(1)} custom-call(f32[1024,128]{1,0:T(8,128)} %bitcast.20, f32[4096,128]{1,0:T(8,128)} %bitcast.18, bf16[8,256,256]{2,1,0:T(8,128)(2,1)} %bitcast.19, bf16[6,256,256]{2,1,0:T(8,128)(2,1)} %constant.2.clone.tab_hbm, s32[1,2,8]{2,1,0:T(2,128)} %bitcast.21, s32[1,1]{1,0:T(1,128)S(6)} %copy.12.cnt_hbm), custom_call_target="tpu_custom_call" | custom-call | flops 5000000000 | bytes 5000000 | tf_op jit(solution)/shard_map/pallas_call | solution.py:600
  29.5 0.8 %copy.11 = f32[256,2,256]{2,1,0:T(2,128)} copy(f32[256,2,256]{2,1,0:T(2,128)S(1)} %bitcast.17) | data formatting | bytes 1048576

commit v6 on v5

--- a/solution.py
+++ b/solution.py
@@ -336,21 +336,23 @@
 
 
     def exit_waves():
-        def piece(first, k):
+        def piece(first):
             cut = slice(first, first + 16)
             at = 2 * first if first < 128 else 2 * (first - 128) + 16
-            waves = []
-            for b in range(2):
-                p_re, p_im, w_re, w_im = pp[k, 0, b, cut, :], pp[k, 1, b, cut, :], win[0, b, cut, :], win[1, b, cut, :]
-                waves.append((p_re * w_re - p_im * w_im, p_re * w_im + p_im * w_re))
-            to_rows = slice(256 * k + at, 256 * k + at + 16)
-            for part in range(2):
-                low, high = waves[0][part], waves[1][part]
-                lanes_of = slice(128 * part, 128 * part + 128)
-                wave[0, to_rows, lanes_of] = (low + high).astype(BF16)
-                wave[1, to_rows, lanes_of] = (low - high).astype(BF16)
-
-        return [functools.partial(piece, first, k) for first in range(0, 256, 16) for k in range(modes)]
+            w_re, w_im = [win[0, b, cut, :] for b in range(2)], [win[1, b, cut, :] for b in range(2)]
+            for k in range(modes):
+                waves = []
+                for b in range(2):
+                    p_re, p_im = pp[k, 0, b, cut, :], pp[k, 1, b, cut, :]
+                    waves.append((p_re * w_re[b] - p_im * w_im[b], p_re * w_im[b] + p_im * w_re[b]))
+                to_rows = slice(256 * k + at, 256 * k + at + 16)
+                for part in range(2):
+                    low, high = waves[0][part], waves[1][part]
+                    lanes_of = slice(128 * part, 128 * part + 128)
+                    wave[0, to_rows, lanes_of] = (low + high).astype(BF16)
+                    wave[1, to_rows, lanes_of] = (low - high).astype(BF16)
+
+        return [functools.partial(piece, first) for first in range(0, 256, 16)]
 
     def half_done():
         done = {}

time: 30.8 us -> 30.4 us (0.987)
  no operation moved by 1% of the time
where the time goes in v6:
time: 30.4 us; the launch traced here: 30.2 us
  Pallas kernels  28.8 us (95%)
  local copies, waits for them, and re-layouts  0.8 us (3%)
  between operations  0.66 us (2%)
    pallas_call x1, Pallas kernels, on_device(): pl.pallas_call(functools.partial(kernel, n_row, n_col, slots, modes), out...  28.8 us
    unnamed x1, local copies, waits for them, and re-layouts  0.8 us

profile of v6, /device:TPU:15, one launch (start us, length us, event | category | flops | bytes accessed | tf_op | source)
XLA Modules:
  0.0 30.2 jit_solution(3511244088349663580)
XLA Ops:
  0.7 28.8 %shard_map.64 = f32[1024,128]{1,0:T(8,128)S(1)} custom-call(f32[1024,128]{1,0:T(8,128)} %bitcast.20, f32[4096,128]{1,0:T(8,128)} %bitcast.18, bf16[8,256,256]{2,1,0:T(8,128)(2,1)} %bitcast.19, bf16[6,256,256]{2,1,0:T(8,128)(2,1)} %constant.2.clone.tab_hbm, s32[1,2,8]{2,1,0:T(2,128)} %bitcast.21, s32[1,1]{1,0:T(1,128)S(6)} %copy.12.cnt_hbm), custom_call_target="tpu_custom_call" | custom-call | flops 5000000000 | bytes 5000000 | tf_op jit(solution)/shard_map/pallas_call | solution.py:602
  29.4 0.8 %copy.11 = f32[256,2,256]{2,1,0:T(2,128)} copy(f32[256,2,256]{2,1,0:T(2,128)S(1)} %bitcast.17) | data formatting | bytes 1048576

commit v7 on v6

--- a/solution.py
+++ b/solution.py
@@ -281,6 +281,9 @@
         return carry
 
     lax.fori_loop(0, 4, weigh, 0)
+    for b in range(4):
+        ws[0, b] = cw[0, b].astype(BF16)
+
     widen(OBJ + 4, [1, 2], outer_rim)
     widen(OBJ + 5, [1, 2], inner_rim)
     for copy, there, block, vertical in corner_copies:
@@ -292,9 +295,9 @@
             for c in range(2):
                 ext[c, block, span, :] = rim[c, block, span, :].astype(F32)
 
-    def halo_out(base, gather, layers, stage, from_inner, from_x, from_corner, from_outer):
+    def halo_out(base, gather, layers, stage, from_inner, from_x, from_corner, from_outer, ready=False):
         def rounded(blocks, span):
-            for c in range(layers):
+            for c in range(0 if ready else layers):
                 for b in blocks:
                     stage[c, b, span, :] = gather(c, b, span).astype(BF16)
 
@@ -319,7 +322,7 @@
     def weight_at(c, b, span):
         return cw[c, b, span, :]
 
-    halo_out(WEIGHT, weight_at, 1, ws, wi, wx, wd, wo)
+    halo_out(WEIGHT, weight_at, 1, ws, wi, wx, wd, wo, True)
 
     def cut_window(j):
         y, x = table[1, j], table[2, j]

time: 30.4 us -> 30.4 us (level)
  no operation moved by 1% of the time
where the time goes in v7:
time: 30.4 us; the launch traced here: 30.2 us
  Pallas kernels  28.8 us (95%)
  local copies, waits for them, and re-layouts  0.8 us (3%)
  between operations  0.66 us (2%)
    pallas_call x1, Pallas kernels, on_device(): pl.pallas_call(functools.partial(kernel, n_row, n_col, slots, modes), out...  28.8 us
    unnamed x1, local copies, waits for them, and re-layouts  0.8 us

profile of v7, /device:TPU:15, one launch (start us, length us, event | category | flops | bytes accessed | tf_op | source)
XLA Modules:
  0.0 30.2 jit_solution(7780738756068108589)
XLA Ops:
  0.7 28.8 %shard_map.64 = f32[1024,128]{1,0:T(8,128)S(1)} custom-call(f32[1024,128]{1,0:T(8,128)} %bitcast.20, f32[4096,128]{1,0:T(8,128)} %bitcast.18, bf16[8,256,256]{2,1,0:T(8,128)(2,1)} %bitcast.19, bf16[6,256,256]{2,1,0:T(8,128)(2,1)} %constant.2.clone.tab_hbm, s32[1,2,8]{2,1,0:T(2,128)} %bitcast.21, s32[1,1]{1,0:T(1,128)S(6)} %copy.12.cnt_hbm), custom_call_target="tpu_custom_call" | custom-call | flops 5000000000 | bytes 5000000 | tf_op jit(solution)/shard_map/pallas_call | solution.py:605
  29.4 0.8 %copy.11 = f32[256,2,256]{2,1,0:T(2,128)} copy(f32[256,2,256]{2,1,0:T(2,128)S(1)} %bitcast.17) | data formatting | bytes 1048576
